TPU v7x, 256 devices: a whole 4x4x8 slice. The times are simulated.
256 devices in a mesh: trace: 64 (over z, x, core), freq: 4 (over y).
Axes of the slice: x: 4, y: 4, z: 8, core: 2. Of those that a mesh axis runs over, the one named last changes fastest.
Arguments:
- traces: float32 [32768, 2048], P('trace'), may hold values from -40 to 40, as said below
- shot_local: int32 [64, 512], P('trace'), may hold values from 0 to 15, never falling along the last dimension, each value on 1 to 64 neighbouring positions
- rec_slot: int32 [64, 512], P('trace'), may hold values from 0 to 255, as said below
- slot_station: int32 [64, 256], P('trace'), may hold values from 0 to 31, as said below
- cmp_owner: int32 [32768, 1], P('trace'), may hold values from 0 to 63; in each aligned block of 512 rows (0 to 511, 512 to 1023, ...) at most 16 rows name the same one
- cmp_local: int32 [32768], P('trace'), may hold values from 0 to 31
Outputs:
- shot_terms: float32 [1024, 1024], P('trace', 'freq')
- receiver_terms: float32 [2048, 1024], P('trace', 'freq')
- cmp_stack: float32 [2048, 2, 1024], P('trace', None, 'freq')
Inputs may be any that keep to these rules, and one draw needn't show every extreme that they name: `shot_local`: every trace of every index of trace falls in one of its 16 shots, and every shot has a trace. `rec_slot`: slot s of an index of trace goes to the owner s // 4; on every index of trace, each slot is used by at least one trace. `slot_station`: the 4 slots of one index of trace towards one owner name distinct stations; every station of every owner is named by some slot. `cmp_owner`: at most 16 traces of one index of trace name the same owner. `traces`: samples lie within the range.
All inputs are finite; a program needn't handle non-finite values.
Results may differ from a plain program's by a relative error of at most 0.0001.
Values sent between devices are 32-bit elements; how exact they have to be, the bound alone decides.
A program may use at most 64 MiB of HBM per device.

v0:
```python
import jax
import jax.numpy as jnp
from jax import lax
from jax.sharding import PartitionSpec as P

SWEEPS = 2


def shards(traces, shot_local, rec_slot, slot_station, cmp_owner, cmp_local):
    nodes = lax.axis_size("trace")
    bands = lax.axis_size("freq")
    tdev, samples = traces.shape
    nbins = samples // 2
    band = nbins // bands
    first_bin = lax.axis_index("freq") * band
    bins = first_bin + jnp.arange(band, dtype=jnp.int32)
    times_idx = jnp.arange(samples, dtype=jnp.int32)
    position = times_idx[:, None] * bins[None, :] % samples
    angle = 2.0 * jnp.pi * position.astype(jnp.float32) / samples
    norm_factor = 1.0 / jnp.sqrt(jnp.float32(samples))
    table = jnp.concatenate([jnp.cos(angle), -jnp.sin(angle)], axis=1) * norm_factor
    spectra = jnp.dot(
        traces, table, precision=lax.Precision.HIGHEST, preferred_element_type=jnp.float32
    )
    real_part = spectra[:, :band]
    imag_part = spectra[:, band:]
    power = real_part * real_part + imag_part * imag_part
    level = lax.psum(jnp.sum(power, axis=1), "freq") / nbins
    logs = jnp.log(power + 0.01 * level[:, None])
    shot_count_dev = tdev // 32
    shot_ids = shot_local[0]
    shot_hot = (shot_ids[:, None] == jnp.arange(shot_count_dev, dtype=jnp.int32)[None, :]).astype(
        jnp.float32
    )
    shot_count = jnp.sum(shot_hot, axis=0)
    slots = rec_slot[0]
    station_row = slot_station[0]
    slot_total = station_row.shape[0]
    cap = slot_total // nodes
    rec_dev = tdev // 16
    rec_global = slots // cap * rec_dev + station_row[slots]
    slot_count = jax.ops.segment_sum(jnp.ones((tdev,), jnp.float32), slots, num_segments=slot_total)
    recv_count, recv_ids = (
        lax.all_to_all(slot_count, "trace", split_axis=0, concat_axis=0, tiled=True),
        lax.all_to_all(
            station_row.astype(jnp.float32), "trace", split_axis=0, concat_axis=0, tiled=True
        ),
    )
    owner_ids = recv_ids.astype(jnp.int32)
    station_count = jax.ops.segment_sum(recv_count, owner_ids, num_segments=rec_dev)
    rec_trace = jnp.zeros((tdev, band), jnp.float32)
    shot_trace = jnp.zeros((tdev, band), jnp.float32)
    shot_terms = jnp.zeros((shot_count_dev, band), jnp.float32)
    receiver_terms = jnp.zeros((rec_dev, band), jnp.float32)
    for sweep in range(SWEEPS):
        shot_sums = jnp.einsum(
            "ts,tf->sf", shot_hot, logs - rec_trace, precision=lax.Precision.HIGHEST
        )
        shot_terms = shot_sums / shot_count[:, None]
        shot_trace = jnp.einsum("ts,sf->tf", shot_hot, shot_terms, precision=lax.Precision.HIGHEST)
        leftover = logs - shot_trace
        count = rec_dev * lax.axis_size("trace")
        local_ids = rec_global
        inside = (local_ids >= 0) & (local_ids < count)
        local_ids = jnp.where(inside, local_ids, count)
        station_sums = lax.psum_scatter(
            jax.ops.segment_sum(leftover, local_ids, num_segments=count + 1)[:count],
            "trace",
            scatter_dimension=0,
            tiled=True,
        )
        receiver_terms = station_sums / station_count[:, None]
        piece = lax.all_gather(receiver_terms, "trace", axis=0, tiled=True)
        rows = piece.shape[0]
        pick_inside = (rec_global >= 0) & (rec_global < rows)
        taken = piece[jnp.clip(rec_global, 0, rows - 1)]
        rec_trace = jnp.where(pick_inside[:, None], taken, 0.0)
    model = shot_trace + rec_trace
    expmodel = jnp.exp(model)
    mean_model = lax.psum(jnp.sum(expmodel, axis=1), "freq") / nbins
    wiener = jnp.exp(0.5 * model) / (expmodel + 0.3 * mean_model[:, None])
    decon = jnp.stack([wiener * real_part, wiener * imag_part], axis=1)
    owner = cmp_owner[:, 0]
    capc = 2 * tdev // nodes
    owner_hot = (owner[:, None] == jnp.arange(nodes, dtype=jnp.int32)[None, :]).astype(jnp.int32)
    before = jnp.cumsum(owner_hot, axis=0) - owner_hot
    rank = jnp.sum(before * owner_hot, axis=1)
    target = owner * capc + rank
    outgoing = jnp.zeros((nodes * capc, 2, band), jnp.float32).at[target].set(decon)
    out_ids = (
        jnp.full((nodes * capc,), -1.0, jnp.float32).at[target].set(cmp_local.astype(jnp.float32))
    )
    incoming, in_ids = (
        lax.all_to_all(outgoing, "trace", split_axis=0, concat_axis=0, tiled=True),
        lax.all_to_all(out_ids, "trace", split_axis=0, concat_axis=0, tiled=True),
    )
    cmp_dev = tdev // 16
    gather_ids = in_ids.astype(jnp.int32)
    gather_ids = jnp.where(gather_ids < 0, cmp_dev, gather_ids)
    cmp_stack = 0.25 * jax.ops.segment_sum(incoming, gather_ids, num_segments=cmp_dev + 1)[:cmp_dev]
    return (shot_terms, receiver_terms, cmp_stack)


def solution(mesh):
    return jax.shard_map(
        shards,
        mesh=mesh,
        in_specs=(
            P("trace", None),
            P("trace", None),
            P("trace", None),
            P("trace", None),
            P("trace", None),
            P("trace"),
        ),
        out_specs=(P("trace", "freq"), P("trace", "freq"), P("trace", None, "freq")),
        check_vma=False,
    )
```

profile of v0, /device:TPU:32, one launch (start us, length us, event | category | flops | bytes accessed | tf_op | source)
XLA Modules:
  0.0 669.1 jit_solution(15968367289181125755)
XLA Ops:
  7.2 8.2 %fusion.15 = (f32[2048,256]{1,0:T(8,128)S(1)}, f32[2048,256]{1,0:T(8,128)S(1)}) fusion(s32[256]{0:T(256)S(1)} %iota_add_fusion), kind=kLoop, calls=%fused_computation.34 | loop fusion | flops 7864320 | bytes 4195328 | tf_op jit(solution)/shard_map/cos | solution.py:21
  15.5 13.8 %fusion.10 = f32[512,512]{0,1:T(8,128)S(1)} fusion(f32[512,2048]{1,0:T(8,128)S(1)} %copy-done.2, f32[2048,256]{1,0:T(8,128)S(1)} %get-tuple-element.10, f32[2048,256]{1,0:T(8,128)S(1)} %get-tuple-element.9), kind=kOutput, calls=%fused_computation.25 | convolution fusion | flops 6444548096 | bytes 9437184 | tf_op jit(solution)/shard_map/dot_general | solution.py:22
  29.4 10.9 %psum.14 = f32[512]{0:T(512)S(1)} all-reduce(f32[512]{0:T(512)S(1)} %get-tuple-element.5), channel_id=1, replica_groups=mesh['trace'=64,'freq'=4] {'freq'}, use_global_device_ids=true, to_apply=%region_1.2 | all-reduce | flops 512 | bytes 4096 | tf_op jit(solution)/shard_map/psum | solution.py:28
  40.5 0.4 convolution_divide_fusion.1
  40.9 0.5 convolution_subtract_fusion
  41.4 0.2 copy.28
  41.6 3.5 gather_fusion
  45.2 4.7 scatter_custom_fusion
  49.9 3.1 slice.36
  53.0 4.1 scatter_custom_fusion.1
  57.1 0.7 all_to_all.22
  57.8 11.6 %all-to-all-start.1 = ((f32[64,4,1]{1,2,0:T(1,128)}), f32[64,4,1]{1,2,0:T(1,128)S(1)}, u32[]{:S(2)}, u32[]{:S(2)}) async-start(f32[64,4,1]{1,2,0:T(1,128)} %bitcast.9), calls=%async_computation.2 | async-start | bytes 65536 | tf_op jit(solution)/shard_map/all_to_all | solution.py:44
  69.4 0.7 convert_element_type.58
  70.2 7.8 %all-to-all-done.1 = f32[64,4,1]{1,2,0:T(1,128)S(1)} async-done(((f32[64,4,1]{1,2,0:T(1,128)}), f32[64,4,1]{1,2,0:T(1,128)S(1)}, u32[]{:S(2)}, u32[]{:S(2)}) %all-to-all-start.1) | async-done | bytes 1056 | tf_op jit(solution)/shard_map/all_to_all | solution.py:44
  78.0 5.5 all-to-all-start
  83.5 0.5 broadcast.296
  84.0 0.7 reduce.17
  84.9 7.2 %all-to-all-done = f32[64,4,1]{1,2,0:T(1,128)S(1)} async-done(((f32[64,4,1]{1,2,0:T(1,128)}), f32[64,4,1]{1,2,0:T(1,128)S(1)}, u32[]{:S(2)}, u32[]{:S(2)}) %all-to-all-start) | async-done | bytes 1056 | tf_op jit(solution)/shard_map/all_to_all | solution.py:45
  92.3 2.3 scatter_custom_fusion.2
  94.6 98.5 %reduce-scatter.3.cloned.1.call-done = f32[32,256]{1,0:T(8,128)} async-done(((f32[2048,256]{1,0:T(8,128)}), f32[32,256]{1,0:T(8,128)}) %reduce-scatter.3.cloned.1.call-update) | async-done | bytes 32784 | tf_op jit(solution)/shard_map/reduce_scatter | solution.py:66
  193.1 1.4 broadcast_divide_fusion.1
  194.6 0.3 reduce-scatter.5.cloned.1.call-start
  194.9 77.5 %all-gather.3.cloned.1.call-done = f32[2048,256]{1,0:T(8,128)} async-done(((f32[32,256]{1,0:T(8,128)}), f32[2048,256]{1,0:T(8,128)}) %all-gather.3.cloned.1.call-update) | async-done | bytes 2097168 | tf_op jit(solution)/shard_map/all_gather | solution.py:73
  272.3 3.2 gather_fusion.1
  275.5 0.2 copy.31
  275.7 0.5 convolution_divide_fusion
  276.2 1.2 fusion.18
  277.4 1.0 copy.32
  278.4 4.3 scatter_custom_fusion.3
  282.7 1.5 slice.37
  284.3 138.5 %reduce-scatter.5.cloned.1.call-done = f32[32,256]{1,0:T(8,128)} async-done(((f32[2048,256]{1,0:T(8,128)}), f32[32,256]{1,0:T(8,128)}) %reduce-scatter.5.cloned.1.call-update) | async-done | bytes 32784 | tf_op jit(solution)/shard_map/reduce_scatter | solution.py:66
  422.8 1.4 broadcast_divide_fusion
  424.3 1.2 reduce-window.6
  425.5 0.2 slice_reduce_fusion
  425.9 2.4 scatter_custom_fusion.4
  428.4 0.7 all_to_all.25
  429.1 8.4 %all-to-all-start.2 = ((f32[64,16,1]{1,2,0:T(1,128)}), f32[64,16,1]{1,2,0:T(1,128)S(1)}, u32[]{:S(2)}, u32[]{:S(2)}) async-start(f32[64,16,1]{1,2,0:T(1,128)} %bitcast.16), calls=%async_computation.4 | async-start | bytes 65536 | tf_op jit(solution)/shard_map/all_to_all | solution.py:95
  437.5 64.1 %all-gather.5.cloned.1.call-done = f32[2048,256]{1,0:T(8,128)} async-done(((f32[32,256]{1,0:T(8,128)}), f32[2048,256]{1,0:T(8,128)}) %all-gather.5.cloned.1.call-update) | async-done | bytes 2097168 | tf_op jit(solution)/shard_map/all_gather | solution.py:73
  501.6 3.2 gather_fusion.2
  505.1 10.5 %psum.15 = f32[512]{0:T(512)S(1)} all-reduce(f32[512]{0:T(512)S(1)} %exponential_reduce_fusion), channel_id=1, replica_groups=mesh['trace'=64,'freq'=4] {'freq'}, use_global_device_ids=true, to_apply=%region_14.15 | all-reduce | flops 512 | bytes 4096 | tf_op jit(solution)/shard_map/psum | solution.py:80
  515.6 0.2 multiply_bitcast_fusion.1
  515.9 0.6 copy.36
  516.5 1.9 broadcast_in_dim.70
  518.4 47.4 %scatter_fusion = f32[1024,2,256]{2,1,0:T(2,128)} fusion(f32[1024,2,256]{2,1,0:T(2,128)} %broadcast_in_dim.70, s32[512]{0:T(512)S(1)} %bitcast.72, f32[512,2,256]{2,1,0:T(2,128)S(1)} %copy.36), kind=kCustom, calls=%fused_computation.8 | custom fusion | bytes 3147776 | tf_op jit(solution)/shard_map/scatter | solution.py:89
  565.8 8.0 %all-to-all-start.3 = ((f32[1024,2,256]{2,1,0:T(2,128)}), f32[1024,2,256]{2,1,0:T(2,128)S(1)}, u32[]{:S(2)}, u32[]{:S(2)}) async-start(f32[1024,2,256]{2,1,0:T(2,128)} %scatter_fusion), calls=%async_computation.5 | async-start | bytes 4194304 | tf_op jit(solution)/shard_map/all_to_all | solution.py:94
  574.0 50.2 %all-to-all-done.3 = f32[1024,2,256]{2,1,0:T(2,128)S(1)} async-done(((f32[1024,2,256]{2,1,0:T(2,128)}), f32[1024,2,256]{2,1,0:T(2,128)S(1)}, u32[]{:S(2)}, u32[]{:S(2)}) %all-to-all-start.3) | async-done | bytes 2097184 | tf_op jit(solution)/shard_map/all_to_all | solution.py:94
  624.2 37.5 %scatter_fusion.1 = f32[33,2,256]{2,1,0:T(2,128)S(1)} fusion(f32[33,2,256]{2,1,0:T(2,128)S(1)} %broadcast_in_dim.67, s32[1024]{0:T(1024)S(1)} %bitcast.67, f32[1024,2,256]{2,1,0:T(2,128)S(1)} %all-to-all-done.3), kind=kCustom, calls=%fused_computation.9 | custom fusion | flops 524288 | bytes 6295552 | tf_op jit(solution)/shard_map/scatter-add | solution.py:100
  661.7 0.7 slice_multiply_fusion
  (53 shorter events, 1.7 us)
Async XLA Ops:
  7.2 185.9 %reduce-scatter.3.cloned.1.call-start = ((), (), s32[]{:S(2)}) async-start(), calls=%async_computation.6 | async-start | bytes 2129920 | tf_op jit(solution)/shard_map/reduce_scatter | solution.py:66
  7.2 8.3 %copy-start.2 = (f32[512,2048]{1,0:T(8,128)S(1)}, f32[512,2048]{1,0:T(8,128)}, u32[]{:S(2)}) copy-start(f32[512,2048]{1,0:T(8,128)} %param.6) | copy-start | bytes 12582916
  15.5 24.9 %copy-start.4 = (s32[1,512]{1,0:T(1,128)S(1)}, s32[1,512]{1,0:T(1,128)}, u32[]{:S(2)}) copy-start(s32[1,512]{1,0:T(1,128)} %param.7) | copy-start | bytes 6148
  29.3 12.3 %copy-start.6 = (s32[1,512]{1,0:T(1,128)S(1)}, s32[1,512]{1,0:T(1,128)}, u32[]{:S(2)}) copy-start(s32[1,512]{1,0:T(1,128)} %param.8) | copy-start | bytes 6148
  29.3 12.3 %copy-start = (s32[1,256]{1,0:T(1,128)S(1)}, s32[1,256]{1,0:T(1,128)}, u32[]{:S(2)}) copy-start(s32[1,256]{1,0:T(1,128)} %param.9) | copy-start | bytes 3076
  57.8 20.1 %all-to-all-start.1 = ((f32[64,4,1]{1,2,0:T(1,128)}), f32[64,4,1]{1,2,0:T(1,128)S(1)}, u32[]{:S(2)}, u32[]{:S(2)}) async-start(f32[64,4,1]{1,2,0:T(1,128)} %bitcast.9), calls=%async_computation.2 | async-start | bytes 65536 | tf_op jit(solution)/shard_map/all_to_all | solution.py:44
  78.0 14.1 %all-to-all-start = ((f32[64,4,1]{1,2,0:T(1,128)}), f32[64,4,1]{1,2,0:T(1,128)S(1)}, u32[]{:S(2)}, u32[]{:S(2)}) async-start(f32[64,4,1]{1,2,0:T(1,128)} %bitcast.8), calls=%async_computation.1 | async-start | bytes 65536 | tf_op jit(solution)/shard_map/all_to_all | solution.py:45
  83.5 188.9 %all-gather.3.cloned.1.call-start = ((), (), s32[]{:S(2)}) async-start(), calls=%async_computation.7 | async-start | bytes 2129920 | tf_op jit(solution)/shard_map/all_gather | solution.py:73
  194.6 228.2 %reduce-scatter.5.cloned.1.call-start = ((), (), s32[]{:S(2)}) async-start(), calls=%async_computation.8 | async-start | bytes 2129920 | tf_op jit(solution)/shard_map/reduce_scatter | solution.py:66
  276.2 6.6 copy-start.3
  284.2 140.1 %copy-start.5 = (s32[512,1]{0,1:T(1,128)S(1)}, s32[512,1]{0,1:T(1,128)}, u32[]{:S(2)}) copy-start(s32[512,1]{0,1:T(1,128)} %param.10) | copy-start | bytes 6148
  284.2 141.6 %copy-start.7 = (s32[512]{0:T(512)S(1)}, s32[512]{0:T(512)}, u32[]{:S(2)}) copy-start(s32[512]{0:T(512)} %param.11) | copy-start | bytes 6148
  284.2 217.4 %all-gather.5.cloned.1.call-start = ((), (), s32[]{:S(2)}) async-start(), calls=%async_computation.9 | async-start | bytes 2129920 | tf_op jit(solution)/shard_map/all_gather | solution.py:73
  429.1 136.7 %all-to-all-start.2 = ((f32[64,16,1]{1,2,0:T(1,128)}), f32[64,16,1]{1,2,0:T(1,128)S(1)}, u32[]{:S(2)}, u32[]{:S(2)}) async-start(f32[64,16,1]{1,2,0:T(1,128)} %bitcast.16), calls=%async_computation.4 | async-start | bytes 65536 | tf_op jit(solution)/shard_map/all_to_all | solution.py:95
  437.5 67.4 %copy-start.1 = (f32[512,256]{0,1:T(8,128)S(1)}, f32[512,256]{0,1:T(8,128)}, u32[]{:S(2)}) copy-start(f32[512,256]{0,1:T(8,128)} %get-tuple-element.12) | copy-start | bytes 1572868
  565.8 58.4 %all-to-all-start.3 = ((f32[1024,2,256]{2,1,0:T(2,128)}), f32[1024,2,256]{2,1,0:T(2,128)S(1)}, u32[]{:S(2)}, u32[]{:S(2)}) async-start(f32[1024,2,256]{2,1,0:T(2,128)} %scatter_fusion), calls=%async_computation.5 | async-start | bytes 4194304 | tf_op jit(solution)/shard_map/all_to_all | solution.py:94
Sparse Core Ops, SparseCore 0:
  53.1 139.9 reduce-scatter.2
  196.8 75.4 all-gather.2
  284.4 138.4 reduce-scatter.4
  426.0 75.5 all-gather.4
where the time goes:
time: 680 us; the launch traced here: 669 us
  waiting for transfers between devices  444 us (65%)
  local copies, waits for them, and re-layouts  71.5 us (11%)
  other arithmetic  67.8 us (10%)
  starting transfers between devices  33.9 us (5%)
  blocking collectives  21.4 us (3%)
  matrix products  16.4 us (2%)
  between operations  14.4 us (2%)
    reduce_scatter x2, waiting for transfers between devices, shards(): lax.psum_scatter(jax.ops.segment_sum(leftover, local_ids, num_segments=co...  237 us
    all_gather x2, waiting for transfers between devices, shards(): piece = lax.all_gather(receiver_terms, 'trace', axis=0, tiled=True)  142 us
    all_to_all x1, waiting for transfers between devices, shards(): lax.all_to_all(outgoing, 'trace', split_axis=0, concat_axis=0, tiled=True)  50.2 us
    scatter x1, local copies, waits for them, and re-layouts, shards(): jnp.zeros((nodes * capc, 2, band), jnp.float32).at[target].set(decon)  47.4 us
    scatter-add x1, other arithmetic, shards(): jax.ops.segment_sum(incoming, gather_ids, num_segments=cmp_dev + 1)  37.5 us
    dot_general x1, matrix products, shards(): jnp.dot(traces, table, precision=lax.Precision.HIGHEST, preferred_element...  13.8 us
  transfers between devices with their start and end apart: 8, of which 7 were waited for; matrix products, arithmetic and copies ran while one was open for 10% of the time, Pallas kernels for 0%

commit v1 on v0

v1 whole, which is shorter than its diff:
```python
import functools

import jax
import jax.numpy as jnp
import numpy as np
from jax import lax
from jax.experimental import pallas as pl
from jax.experimental.pallas import tpu as pltpu
from jax.sharding import PartitionSpec as P

NT = 2048
HALF = 1024
NB = 128
TDEV = 512
ROWS = 512
F32 = jnp.float32
BF16 = jnp.bfloat16
NT_DIMS = (((1,), (1,)), ((), ()))
TN_DIMS = (((0,), (0,)), ((), ()))


def twiddles():
    bins = np.arange(4)[:, None, None] * 256 + np.arange(2)[None, :, None] + 2 * np.arange(NB)[None, None, :]
    low = -2.0 * np.pi * ((np.arange(128)[:, None] * bins[:, :, None, :]) % NT) / NT
    high = -2.0 * np.pi * ((128 * np.arange(8)[:, None] * bins[:, :, None, :]) % NT) / NT
    norm = NT**-0.5
    low = np.concatenate([np.cos(low), np.sin(low)], axis=-1) * norm
    high = np.concatenate([np.cos(high), np.sin(high)], axis=-1)
    return low.astype(np.float32), high.astype(np.float32)


def split(x, parts):
    out = []
    for i in range(parts):
        piece = x.astype(BF16)
        out.append(piece)
        if i + 1 < parts:
            x = x - piece.astype(F32)
    return out


def hot_dot(hot, x, parts=3, dims=(((1,), (0,)), ((), ()))):
    n = x.shape[1]
    full = lax.dot_general(hot, jnp.concatenate(split(x, parts), axis=1), dims, preferred_element_type=F32)
    total = full[:, :n]
    for i in range(1, parts):
        total = total + full[:, i * n:(i + 1) * n]
    return total


def iota(shape, axis):
    return lax.broadcasted_iota(jnp.int32, shape, axis)


def hot(condition):
    return jnp.where(condition, 1.0, 0.0).astype(BF16)


def kernel(
    traces, index, low_tab, high_tab,
    shot_out, rec_out, cmp_out,
    xbuf, low, high, table, uhi, ulo, vhi, vlo, level, spec, logs,
    slot_rows, slot_cols, shot_rows, shot_cols, cmp_hot, owner_cols,
    meta_send, meta_recv, sum_send, sum_recv, term_send, term_recv, q_send, q_recv,
    dense, rs0, rs1, rs2, rs3,
    x_sem, tab_sem, a2a_send, a2a_recv, q_ssem, q_rsem, rs_send, rs0_sem, rs1_sem, rs2_sem, rs3_sem,
):
    me = lax.axis_index("trace")
    band = lax.axis_index("freq")
    z = lax.div(me, 8)
    x = lax.rem(lax.div(me, 2), 4)
    core = lax.rem(me, 2)

    barrier = pltpu.get_barrier_semaphore()

    @pl.loop(1, 64)
    def _(p):
        pl.semaphore_signal(barrier, inc=1, device_id={"trace": lax.rem(me + p, 64)})

    for p in range(1, 4):
        pl.semaphore_signal(barrier, inc=1, device_id={"freq": lax.rem(band + p, 4)})

    def x_copy(c):
        rows = pl.ds(c * 64, 64)
        return pltpu.make_async_copy(traces.at[rows], xbuf.at[rows], x_sem.at[c])

    low_copy = pltpu.make_async_copy(low_tab.at[band], low, tab_sem.at[0])
    high_copy = pltpu.make_async_copy(high_tab.at[band], high, tab_sem.at[1])
    low_copy.start()
    high_copy.start()
    for c in range(8):
        x_copy(c).start()

    by_lane = index[...]
    by_row = jnp.transpose(by_lane)
    shot_lane, slot_lane, cmp_lane, station_lane = (by_lane[i:i + 1, :] for i in range(4))
    shot_row, slot_row = by_row[:, 0:1], by_row[:, 1:2]

    i0 = iota((ROWS, TDEV), 0)
    slot_of = (lax.shift_right_logical(i0, 3) * 4 + (i0 & 3)).astype(F32)
    half_of = lax.shift_right_logical(i0, 2) & 1
    same = slot_of == slot_lane
    for h in range(2):
        slot_rows[:, h * TDEV:(h + 1) * TDEV] = hot(same & (half_of == h))
    count = jnp.sum(jnp.where(same, 1.0, 0.0), axis=1, keepdims=True)
    station = jnp.sum(jnp.where(slot_of == iota((ROWS, TDEV), 1).astype(F32), station_lane, 0.0), axis=1, keepdims=True)
    meta_send[...] = jnp.where(iota((ROWS, NB), 1) < 64, station, count)

    i1 = iota((TDEV, ROWS), 1)
    slot_of = (lax.shift_right_logical(i1, 3) * 4 + (i1 & 3)).astype(F32)
    half_of = lax.shift_right_logical(i1, 2) & 1
    same = slot_of == slot_row
    for h in range(2):
        slot_cols[h * TDEV:(h + 1) * TDEV, :] = hot(same & (half_of == h))

    j0, j1 = iota((32, TDEV), 0).astype(F32), iota((TDEV, 32), 1).astype(F32)
    for h in range(2):
        shot_rows[:, h * TDEV:(h + 1) * TDEV] = hot(j0 == shot_lane + 16.0 * h)
        shot_cols[h * TDEV:(h + 1) * TDEV, :] = hot(j1 == shot_row + 16.0 * h)

    def exchange(phase, source, target):
        mine = pl.ds(pl.multiple_of(me * 8, 8), 8)
        target[mine, :] = source[mine, :]

        @pl.loop(1, 64)
        def _(p):
            other = lax.rem(me + p, 64)
            pltpu.make_async_remote_copy(
                src_ref=source.at[pl.ds(pl.multiple_of(other * 8, 8), 8)],
                dst_ref=target.at[mine],
                send_sem=a2a_send.at[phase],
                recv_sem=a2a_recv.at[phase],
                device_id={"trace": other},
            ).start()

    def arrived(phase, target):
        rows = pl.ds(0, 504)
        pltpu.make_async_copy(target.at[rows], target.at[rows], a2a_recv.at[phase]).wait()

    def sent(phase, source):
        rows = pl.ds(0, 504)
        pltpu.make_async_copy(source.at[rows], source.at[rows], a2a_send.at[phase]).wait()

    pl.semaphore_wait(barrier, 66)
    exchange(0, meta_send, meta_recv)

    low_copy.wait()
    high_copy.wait()
    for h in range(2):
        low_re, low_im = low[h, :, :NB], low[h, :, NB:]
        for n1 in range(8):
            high_re, high_im = high[h, n1:n1 + 1, :NB], high[h, n1:n1 + 1, NB:]
            re_hi, re_lo = split(low_re * high_re - low_im * high_im, 2)
            im_hi, im_lo = split(low_re * high_im + low_im * high_re, 2)
            table[h, n1 * 128:(n1 + 1) * 128, :] = jnp.concatenate([re_hi, im_hi, re_lo, im_lo], axis=1)

    sign = 1.0 - 2.0 * (iota((1, HALF), 1) & 1).astype(F32)
    for part in range(2):
        @pl.loop(0, 4)
        def _(b):
            c = part * 4 + b
            x_copy(c).wait()
            rows = pl.ds(pl.multiple_of(c * 64, 64), 64)
            first, second = xbuf[rows, :HALF], xbuf[rows, HALF:]
            u, v = first + second, first - second
            nyquist = jnp.sum(u * sign, axis=1, keepdims=True) * (1.0 / HALF)
            rest = u - nyquist * sign
            energy = jnp.sum(rest * rest + v * v, axis=1, keepdims=True) * 0.5
            mean = jnp.sum(u, axis=1, keepdims=True)
            level[rows, :] = jnp.broadcast_to((energy + mean * mean * (1.0 / NT)) * (0.5 / 1024.0), (64, NB))
            uhi[rows, :], ulo[rows, :] = split(u, 2)
            vhi[rows, :], vlo[rows, :] = split(v, 2)

        rows = slice(part * 256, (part + 1) * 256)
        floor = 0.01 * level[rows, :]
        for h, (hi, lo) in enumerate(((uhi, ulo), (vhi, vlo))):
            full = jnp.dot(hi[rows, :], table[h], preferred_element_type=F32)
            rest = jnp.dot(lo[rows, :], table[h, :, :256], preferred_element_type=F32)
            both = full[:, :256] + (full[:, 256:] + rest)
            spec[rows, h * 256:(h + 1) * 256] = both
            re, im = both[:, :NB], both[:, NB:]
            logs[h * TDEV + part * 256:h * TDEV + (part + 1) * 256, :] = jnp.log(re * re + im * im + floor)

    shots, slots = shot_rows[...], slot_rows[...]
    shot_count = jnp.sum(shots.astype(F32), axis=1, keepdims=True)
    counts = lax.dot_general(shots, slots, NT_DIMS, preferred_element_type=F32).astype(BF16)
    counts_t = lax.dot_general(slots, shots, NT_DIMS, preferred_element_type=F32).astype(BF16)
    shot_sums = hot_dot(shots, logs[...])
    slot_sums = hot_dot(slots, logs[...])

    shot_terms = shot_sums / shot_count
    sum_send[0] = slot_sums - hot_dot(counts_t, shot_terms)
    exchange(1, sum_send.at[0], sum_recv.at[0])

    arrived(0, meta_recv)
    stations = meta_recv[:, 0:64]
    k1 = iota((ROWS, 64), 1)
    k0 = lax.shift_right_logical(iota((ROWS, 64), 0), 2) & 1
    owner_cols[...] = hot((stations == (k1 & 31).astype(F32)) & (k0 == lax.shift_right_logical(k1, 5)))
    owner = owner_cols[...]
    incoming = jnp.broadcast_to(meta_recv[:, 64:65], (ROWS, NB))
    station_count = hot_dot(owner, incoming, 2, TN_DIMS)

    for c in range(8):
        rows = slice(c * 256, (c + 1) * 256)
        cmp_hot[rows, :] = hot((iota((256, TDEV), 0) + c * 256).astype(F32) == cmp_lane)

    for sweep in range(2):
        arrived(1 + 2 * sweep, sum_recv.at[sweep])
        terms = hot_dot(owner, sum_recv[sweep], 3, TN_DIMS) / station_count
        term_send[sweep] = hot_dot(owner, terms)
        exchange(2 + 2 * sweep, term_send.at[sweep], term_recv.at[sweep])
        if sweep == 0:
            arrived(2, term_recv.at[0])
            shot_terms = (shot_sums - hot_dot(counts, term_recv[0])) / shot_count
            sum_send[1] = slot_sums - hot_dot(counts_t, shot_terms)
            exchange(3, sum_send.at[1], sum_recv.at[1])
    rec_out[...] = terms
    shot_out[...] = shot_terms
    shot_part = hot_dot(shot_cols[...], shot_terms)
    arrived(4, term_recv.at[1])
    model = shot_part + hot_dot(slot_cols[...], term_recv[1])
    root = jnp.exp(0.5 * model)
    logs[...] = root
    both = root[:TDEV] * root[:TDEV] + root[TDEV:] * root[TDEV:]
    ones = jnp.ones((8, NB), BF16)
    partial = jnp.zeros((8, TDEV), F32)
    for piece in split(both, 3):
        partial = partial + lax.dot_general(ones, piece, NT_DIMS, preferred_element_type=F32)
    q_send[...] = partial
    q_recv[band] = partial
    q_copies = []
    for p in range(1, 4):
        copy = pltpu.make_async_remote_copy(
            src_ref=q_send, dst_ref=q_recv.at[band], send_sem=q_ssem.at[p - 1], recv_sem=q_rsem.at[p - 1],
            device_id={"freq": lax.rem(band + p, 4)},
        )
        copy.start()
        q_copies.append(copy)
    for copy in q_copies:
        copy.wait()
    total = (q_recv[0] + q_recv[1]) + (q_recv[2] + q_recv[3])
    floor = jnp.broadcast_to(jnp.transpose(total)[:, 0:1], (TDEV, NB)) * (0.3 / 1024.0)
    for h in range(2):
        root = logs[h * TDEV:(h + 1) * TDEV, :]
        wiener = root / (root * root + floor)
        for c in range(2):
            cols = slice((2 * h + c) * NB, (2 * h + c + 1) * NB)
            spec[:, cols] = wiener * spec[:, cols]

    other_half = pl.ds(pl.multiple_of((1 - core) * 1024, 1024), 1024)
    own_half = pl.ds(pl.multiple_of(core * 1024, 1024), 1024)

    def stack(g, half):
        parts = jnp.concatenate(split(spec[:, g * NB:(g + 1) * NB], 2), axis=1)
        full = jnp.dot(cmp_hot[half, :], parts, preferred_element_type=F32)
        return full[:, :NB] + full[:, NB:]

    sibling = {"trace": me + 1 - 2 * core}

    def at_x(step):
        return {"trace": z * 8 + lax.rem(x + step, 4) * 2 + core}

    def x_rows(step, first, size):
        return pl.ds(pl.multiple_of(core * 1024 + lax.rem(x + step, 4) * 256 + first, 128), size)

    def send(src, dst, stage, sem, to):
        return pltpu.make_async_remote_copy(
            src_ref=src, dst_ref=dst, send_sem=rs_send.at[stage], recv_sem=sem, device_id=to
        )

    def step0(g):
        return send(dense.at[g, other_half], rs0.at[g], 0, rs0_sem.at[g], sibling)

    def step1(g, d):
        return send(dense.at[g, x_rows(2, 128 * d, 128)], rs1.at[g, d], 1, rs1_sem.at[g, d], at_x(1 + 2 * d))

    def step2(g, d):
        return send(dense.at[g, x_rows(1 + 2 * d, 0, 256)], rs2.at[g, d], 2, rs2_sem.at[g, d], at_x(1 + 2 * d))

    def begin(g):
        dense[g, other_half, :] = stack(g, other_half)
        step0(g).start()
        dense[g, own_half, :] = stack(g, own_half)

    def after0(g):
        step0(g).wait_recv()
        dense[g, own_half, :] = dense[g, own_half, :] + rs0[g]
        for d in range(2):
            step1(g, d).start()

    def after1(g):
        for d in range(2):
            step1(g, d).wait_recv()
            rows = x_rows(1 + 2 * d, 128 * d, 128)
            dense[g, rows, :] = dense[g, rows, :] + rs1[g, d]
            step2(g, d).start()

    def after2(g):
        mine = x_rows(0, 0, 256)
        for d in range(2):
            step2(g, d).wait_recv()
        dense[g, mine, :] = dense[g, mine, :] + (rs2[g, 0] + rs2[g, 1])
        own = pl.ds(pl.multiple_of(z * 32, 32), 32)
        first = pl.multiple_of(core * 1024 + x * 256, 256)
        rs3[g, own, :] = dense[g, pl.ds(first + z * 32, 32), :]

        @pl.loop(1, 8)
        def _(p):
            there = lax.rem(z + p, 8)
            send(
                dense.at[g, pl.ds(pl.multiple_of(first + there * 32, 32), 32)], rs3.at[g, own],
                3, rs3_sem.at[g], {"trace": there * 8 + x * 2 + core},
            ).start()

    def after3(g):
        rows = pl.ds(0, 224)
        pltpu.make_async_copy(rs3.at[g, rows], rs3.at[g, rows], rs3_sem.at[g]).wait()
        total = rs3[g, 0:32, :]
        for s in range(1, 8):
            total = total + rs3[g, s * 32:(s + 1) * 32, :]
        cmp_out[g] = 0.25 * total

    for step in range(8):
        for offset, stage in ((0, begin), (1, after0), (2, after1), (3, after2), (4, after3)):
            if 0 <= step - offset < 4:
                stage(step - offset)

    sent(0, meta_send)
    for sweep in range(2):
        sent(1 + 2 * sweep, sum_send.at[sweep])
        sent(2 + 2 * sweep, term_send.at[sweep])
    for stage, ref in (
        (0, dense.at[:, pl.ds(0, 1024)]), (1, dense.at[:, pl.ds(0, 256)]),
        (2, dense.at[:, pl.ds(0, 512)]), (3, dense.at[:, pl.ds(0, 224)]),
    ):
        pltpu.make_async_copy(ref, ref, rs_send.at[stage]).wait()


def shards(low_tab, high_tab, traces, shot_local, rec_slot, slot_station, cmp_owner, cmp_local):
    owner = cmp_owner[:, 0]
    row = (owner % 2) * 1024 + (owner // 2 % 4) * 256 + owner // 8 * 32 + cmp_local
    station = jnp.pad(slot_station, ((0, 0), (0, TDEV - slot_station.shape[1])))
    index = jnp.concatenate([shot_local, rec_slot, row[None, :], station], axis=0).astype(F32)
    index = jnp.concatenate([index, jnp.zeros((4, TDEV), F32)], axis=0)
    vmem = pltpu.VMEM
    dma = pltpu.SemaphoreType.DMA
    shot, rec, cmp = pl.pallas_call(
        kernel,
        out_shape=(
            jax.ShapeDtypeStruct((32, NB), F32),
            jax.ShapeDtypeStruct((64, NB), F32),
            jax.ShapeDtypeStruct((4, 32, NB), F32),
        ),
        in_specs=[
            pl.BlockSpec(memory_space=pl.ANY),
            pl.BlockSpec(memory_space=vmem),
            pl.BlockSpec(memory_space=pl.ANY),
            pl.BlockSpec(memory_space=pl.ANY),
        ],
        out_specs=(pl.BlockSpec(memory_space=vmem),) * 3,
        scratch_shapes=[
            vmem((TDEV, NT), F32), vmem((2, 128, 256), F32), vmem((2, 8, 256), F32), vmem((2, HALF, 512), BF16),
            vmem((TDEV, HALF), BF16), vmem((TDEV, HALF), BF16), vmem((TDEV, HALF), BF16), vmem((TDEV, HALF), BF16),
            vmem((TDEV, NB), F32), vmem((TDEV, 512), F32), vmem((2 * TDEV, NB), F32),
            vmem((ROWS, 2 * TDEV), BF16), vmem((2 * TDEV, ROWS), BF16),
            vmem((32, 2 * TDEV), BF16), vmem((2 * TDEV, 32), BF16),
            vmem((2048, TDEV), BF16), vmem((ROWS, 64), BF16),
            vmem((ROWS, NB), F32), vmem((ROWS, NB), F32),
            vmem((2, ROWS, NB), F32), vmem((2, ROWS, NB), F32), vmem((2, ROWS, NB), F32), vmem((2, ROWS, NB), F32),
            vmem((8, TDEV), F32), vmem((4, 8, TDEV), F32),
            vmem((4, 2048, NB), F32), vmem((4, 1024, NB), F32), vmem((4, 2, 128, NB), F32),
            vmem((4, 2, 256, NB), F32), vmem((4, 256, NB), F32),
            dma((8,)), dma((2,)), dma((5,)), dma((5,)), dma((3,)), dma((3,)),
            dma((4,)), dma((4,)), dma((4, 2)), dma((4, 2)), dma((4,)),
        ],
        compiler_params=pltpu.CompilerParams(
            collective_id=0, has_side_effects=True, vmem_limit_bytes=56 * 1024 * 1024
        ),
    )(traces, index, low_tab, high_tab)

    def interleave(a, b):
        return jnp.stack([a, b], axis=-1).reshape(a.shape[:-1] + (2 * NB,))

    return (
        interleave(shot[:16], shot[16:]),
        interleave(rec[:32], rec[32:]),
        interleave(jnp.stack([cmp[0], cmp[1]], axis=1), jnp.stack([cmp[2], cmp[3]], axis=1)),
    )


def solution(mesh):
    low, high = twiddles()
    body = jax.shard_map(
        shards,
        mesh=mesh,
        in_specs=(
            P(), P(),
            P("trace", None),
            P("trace", None),
            P("trace", None),
            P("trace", None),
            P("trace", None),
            P("trace"),
        ),
        out_specs=(P("trace", "freq"), P("trace", "freq"), P("trace", None, "freq")),
        check_vma=False,
    )
    return functools.partial(body, low, high)
```

time: 680 us -> 102 us (0.15); the launches traced: 669 us -> 101 us
  waiting for transfers between devices: 444 us -> 0 us
  Pallas kernels: 0 us -> 93.3 us
  other arithmetic: 67.8 us -> 1.47 us
  local copies, waits for them, and re-layouts: 71.5 us -> 5.34 us
  starting transfers between devices: 33.9 us -> 0 us
  blocking collectives: 21.4 us -> 0 us
  matrix products: 16.4 us -> 0 us
  between operations: 14.4 us -> 0.66 us
    reduce_scatter x2 -> x0, waiting for transfers between devices: 237 us -> none  [shards(): lax.psum_scatter(jax.ops.segment_sum(leftover, local_ids, num_segments=co...]
    all_gather x2 -> x0, waiting for transfers between devices: 142 us -> none  [shards(): piece = lax.all_gather(receiver_terms, 'trace', axis=0, tiled=True)]
    pallas_call x0 -> x1, Pallas kernels: none -> 93.3 us  [shards(): pl.pallas_call(kernel, out_shape=(jax.ShapeDtypeStruct((32, NB), F32), ja...]
    all_to_all x4 -> x0, waiting for transfers between devices: 65.2 us -> none  [the longest x1 50.2 us: shards(): lax.all_to_all(outgoing, 'trace', split_axis=0, concat_axis=0, tiled=True)]
    scatter-add x5 -> x0, other arithmetic: 52.9 us -> none  [the longest x1 37.5 us: shards(): jax.ops.segment_sum(incoming, gather_ids, num_segments=cmp_dev + 1)]
    scatter x2 -> x0, local copies, waits for them, and re-layouts: 49.8 us -> none  [the longest x1 47.4 us: shards(): jnp.zeros((nodes * capc, 2, band), jnp.float32).at[target].set(decon)]
    all_to_all x4 -> x0, starting transfers between devices: 33.5 us -> none  [the longest x1 11.6 us: shards(): lax.all_to_all(slot_count, 'trace', split_axis=0, concat_axis=0, tiled=True)]
    psum x2 -> x0, blocking collectives: 21.4 us -> none  [the longest x1 10.9 us: shards(): level = lax.psum(jnp.sum(power, axis=1), 'freq') / nbins]
  transfers between devices with their start and end apart: 8 -> 0, of which waited for: 7 -> 0; matrix products, arithmetic and copies ran while one was open for 10% -> 0% of each run, Pallas kernels for 0% -> 0%
where the time goes in v1:
time: 102 us; the launch traced here: 101 us
  Pallas kernels  93.3 us (91%)
  local copies, waits for them, and re-layouts  5.34 us (5%)
  other arithmetic  1.47 us (1%)
    pallas_call x1, Pallas kernels, shards(): pl.pallas_call(kernel, out_shape=(jax.ShapeDtypeStruct((32, NB), F32), ja...  93.3 us
    unnamed x3, local copies, waits for them, and re-layouts  2.11 us

profile of v1, /device:TPU:32, one launch (start us, length us, event | category | flops | bytes accessed | tf_op | source)
XLA Modules:
  0.0 100.7 jit_solution(4275575204424074897)
XLA Ops:
  0.6 0.7 fusion.4
  1.4 0.7 fusion
  2.1 0.6 concatenate.7.index
  2.7 93.3 %shard_map.103 = (f32[32,128]{1,0:T(8,128)}, f32[64,128]{1,0:T(8,128)}, f32[4,32,128]{2,1,0:T(8,128)}) custom-call(f32[512,2048]{1,0:T(8,128)} %traces.1, f32[8,512]{1,0:T(8,128)} %concatenate.7.index, f32[4,2,128,256]{3,2,1,0:T(8,128)} %constant.60.clone.low_tab, f32[4,2,8,256]{3,2,1,0:T(8,128)} %constant.61.clone.high_tab), custom_call_target="tpu_custom_call" | custom-call | tf_op jit(solution)/shard_map/pallas_call | solution.py:348
  96.0 0.7 slice_bitcast_fusion.7
  96.7 0.7 slice_bitcast_fusion.5
  97.4 0.8 slice_bitcast_fusion.3
  98.2 0.1 copy.12
  98.4 0.7 copy.15
  99.0 0.1 copy.11
  99.2 0.7 copy.14
  99.8 0.2 copy.13
  100.0 0.7 copy.16
  (4 shorter events, 0.0 us)

commit v2 on v1

v2 whole, which is shorter than its diff:
```python
import functools

import jax
import jax.numpy as jnp
import numpy as np
from jax import lax
from jax.experimental import pallas as pl
from jax.experimental.pallas import tpu as pltpu
from jax.sharding import PartitionSpec as P

NT = 2048
HALF = 1024
NB = 128
TDEV = 512
SLOTS = 256
F32 = jnp.float32
BF16 = jnp.bfloat16
NT_DIMS = (((1,), (1,)), ((), ()))
TN_DIMS = (((0,), (0,)), ((), ()))


def twiddles():
    bins = np.arange(4)[:, None, None] * 256 + np.arange(2)[None, :, None] + 2 * np.arange(NB)[None, None, :]
    low = -2.0 * np.pi * ((np.arange(128)[:, None] * bins[:, :, None, :]) % NT) / NT
    high = -2.0 * np.pi * ((128 * np.arange(8)[:, None] * bins[:, :, None, :]) % NT) / NT
    norm = NT**-0.5
    low = np.concatenate([np.cos(low), np.sin(low)], axis=-1) * norm
    high = np.concatenate([np.cos(high), np.sin(high)], axis=-1)
    return low.astype(np.float32), high.astype(np.float32)


def split(x, parts):
    out = []
    for i in range(parts):
        piece = x.astype(BF16)
        out.append(piece)
        if i + 1 < parts:
            x = x - piece.astype(F32)
    return out


def hot_dot(hot, x, parts=3, dims=(((1,), (0,)), ((), ()))):
    n = x.shape[1]
    full = lax.dot_general(hot, jnp.concatenate(split(x, parts), axis=1), dims, preferred_element_type=F32)
    total = full[:, :n]
    for i in range(1, parts):
        total = total + full[:, i * n:(i + 1) * n]
    return total


def iota(shape, axis):
    return lax.broadcasted_iota(jnp.int32, shape, axis)


def hot(condition):
    return jnp.where(condition, 1.0, 0.0).astype(BF16)


def kernel(
    traces, shot_in, slot_in, station_in, owner_in, local_in, low_tab, high_tab,
    out,
    xbuf, low, high, table, uhi, ulo, vhi, vlo, level, spec, logs, roots,
    shot_idx, slot_idx, station_idx, owner_idx, local_idx,
    slot_rows, slot_cols, shot_cols, cmp_hot, owner_cols,
    first_send, first_recv, sum_send, sum_recv, term_send, term_recv, q_send, q_recv,
    dense, rs0, rs1, rs2, rs3, stacked,
    x_sem, tab_sem, idx_sem, a2a_send, a2a_recv, q_ssem, q_rsem, rs_send, rs0_sem, rs1_sem, rs2_sem, rs3_sem,
):
    me = lax.axis_index("trace")
    band = lax.axis_index("freq")
    z = lax.div(me, 8)
    x = lax.rem(lax.div(me, 2), 4)
    core = lax.rem(me, 2)
    pending = []

    def x_copy(c):
        rows = pl.ds(c * 64, 64)
        return pltpu.make_async_copy(traces.at[rows], xbuf.at[rows], x_sem.at[c])

    low_copy = pltpu.make_async_copy(low_tab.at[band], low, tab_sem.at[0])
    high_copy = pltpu.make_async_copy(high_tab.at[band], high, tab_sem.at[1])
    index_copies = [
        pltpu.make_async_copy(source, target, idx_sem.at[i])
        for i, (source, target) in enumerate((
            (shot_in, shot_idx), (slot_in, slot_idx), (station_in, station_idx), (owner_in, owner_idx), (local_in, local_idx),
        ))
    ]
    low_copy.start()
    high_copy.start()
    for c in range(8):
        x_copy(c).start()
    for copy in index_copies:
        copy.start()

    barrier = pltpu.get_barrier_semaphore()

    @pl.loop(1, 64)
    def _(p):
        pl.semaphore_signal(barrier, inc=1, device_id={"trace": lax.rem(me + p, 64)})

    for p in range(1, 4):
        pl.semaphore_signal(barrier, inc=1, device_id={"freq": lax.rem(band + p, 4)})

    def exchange(leg, source_of, target):
        sems = dict(send_sem=a2a_send.at[leg], recv_sem=a2a_recv.at[leg])

        def put(other):
            pltpu.make_async_remote_copy(
                src_ref=source_of(other), dst_ref=target(me), device_id={"trace": other}, **sems
            ).start()

        @pl.loop(0, 7)
        def _(k):
            side = 1 - 2 * lax.rem(k, 2)
            there = lax.rem(z + 12 + side * lax.div(k + 1, 2), 8) * 8
            for dx in (2, 1, 3, 0):
                for dc in (1, 0):
                    put(there + lax.rem(x + dx, 4) * 2 + lax.rem(core + dc, 2))

        for dx in (2, 1, 3, 0):
            for dc in (1, 0):
                if dx or dc:
                    put(z * 8 + lax.rem(x + dx, 4) * 2 + lax.rem(core + dc, 2))
        pltpu.make_async_copy(source_of(me), target(me), a2a_recv.at[leg]).start()

    def four(ref):
        return lambda d: ref.at[pl.ds(pl.multiple_of(d * 4, 4), 4)]

    def five(ref):
        return lambda d: ref.at[d, pl.ds(0, 5)]

    def exchange_rows(leg, source, target):
        exchange(leg, four(source), four(target))
        part = source.at[pl.ds(0, 252)]
        pending.append(pltpu.make_async_copy(part, part, a2a_send.at[leg]).wait)

    def arrived(leg, target):
        pltpu.make_async_copy(target, target, a2a_recv.at[leg]).wait()

    low_copy.wait()
    high_copy.wait()
    for h in range(2):
        low_re, low_im = low[h, :, :NB], low[h, :, NB:]
        for n1 in range(8):
            high_re, high_im = high[h, n1:n1 + 1, :NB], high[h, n1:n1 + 1, NB:]
            re_hi, re_lo = split(low_re * high_re - low_im * high_im, 2)
            im_hi, im_lo = split(low_re * high_im + low_im * high_re, 2)
            table[h, n1 * 128:(n1 + 1) * 128, :] = jnp.concatenate([re_hi, im_hi, re_lo, im_lo], axis=1)

    for copy in index_copies:
        copy.wait()
    shot_lane = shot_idx[...]
    slot_lane = slot_idx[...]
    station_lane = station_idx[...].astype(F32)
    slot_rows[...] = hot(iota((SLOTS, TDEV), 0) == slot_lane)
    shots = hot(iota((16, TDEV), 0) == shot_lane)
    slots = slot_rows[...]
    shot_count = jnp.sum(shots.astype(F32), axis=1, keepdims=True)
    counts = lax.dot_general(shots, slots, NT_DIMS, preferred_element_type=F32).astype(BF16)
    counts_t = lax.dot_general(slots, shots, NT_DIMS, preferred_element_type=F32).astype(BF16)
    slot_count = lax.dot_general(jnp.ones((8, TDEV), BF16), slots, NT_DIMS, preferred_element_type=F32)[0:1, :]
    meta = jnp.zeros((64, NB), F32)
    lane = iota((64, NB), 1)
    for c in range(4):
        named = iota((64, SLOTS), 1) == iota((64, SLOTS), 0) * 4 + c
        meta = jnp.where(lane == c, jnp.sum(jnp.where(named, station_lane, 0.0), axis=1, keepdims=True), meta)
        meta = jnp.where(lane == 4 + c, jnp.sum(jnp.where(named, slot_count, 0.0), axis=1, keepdims=True), meta)
    first_send[:, 4:5, :] = meta.reshape(64, 1, NB)

    sign = 1.0 - 2.0 * (iota((1, HALF), 1) & 1).astype(F32)

    @pl.loop(0, 8)
    def _(c):
        x_copy(c).wait()
        rows = pl.ds(pl.multiple_of(c * 64, 64), 64)
        first, second = xbuf[rows, :HALF], xbuf[rows, HALF:]
        u, v = first + second, first - second
        nyquist = jnp.sum(u * sign, axis=1, keepdims=True) * (1.0 / HALF)
        rest = u - nyquist * sign
        energy = jnp.sum(rest * rest + v * v, axis=1, keepdims=True) * 0.5
        mean = jnp.sum(u, axis=1, keepdims=True)
        level[rows, :] = jnp.broadcast_to((energy + mean * mean * (1.0 / NT)) * (0.01 * 0.5 / 1024.0), (64, NB))
        uhi[rows, :], ulo[rows, :] = split(u, 2)
        vhi[rows, :], vlo[rows, :] = split(v, 2)

    shot_sums, slot_sums, shot_terms = [None, None], [None, None], [None, None]
    for h, (hi, lo) in enumerate(((uhi, ulo), (vhi, vlo))):
        for part in range(2):
            rows = slice(part * 256, (part + 1) * 256)
            full = jnp.dot(hi[rows, :], table[h], preferred_element_type=F32)
            rest = jnp.dot(lo[rows, :], table[h, :, :256], preferred_element_type=F32)
            both = full[:, :256] + (full[:, 256:] + rest)
            spec[rows, h * 256:(h + 1) * 256] = both
            re, im = both[:, :NB], both[:, NB:]
            logs[h, rows, :] = jnp.log(re * re + im * im + level[rows, :])
        shot_sums[h] = hot_dot(shots, logs[h])
        slot_sums[h] = hot_dot(slot_rows[...], logs[h])
        shot_terms[h] = shot_sums[h] / shot_count
        sums = slot_sums[h] - hot_dot(counts_t, shot_terms[h])
        if h == 0:
            first_send[:, 0:4, :] = sums.reshape(64, 4, NB)
            pl.semaphore_wait(barrier, 66)
            exchange(0, five(first_send), five(first_recv))
            part = first_send.at[pl.ds(0, 63), pl.ds(0, 5)]
            pending.append(pltpu.make_async_copy(part, part, a2a_send.at[0]).wait)
        else:
            sum_send[0] = sums
            exchange_rows(1, sum_send.at[0], sum_recv.at[0])

    by_row = jnp.transpose(jnp.concatenate(
        [shot_lane.astype(F32), slot_lane.astype(F32), jnp.zeros((6, TDEV), F32)], axis=0
    ))
    shot_cols[...] = hot(iota((TDEV, 16), 1).astype(F32) == by_row[:, 0:1])
    slot_cols[...] = hot(iota((TDEV, SLOTS), 1).astype(F32) == by_row[:, 1:2])

    part = first_recv.at[:, pl.ds(0, 5)]
    pltpu.make_async_copy(part, part, a2a_recv.at[0]).wait()
    of_source = hot(lax.shift_right_logical(iota((SLOTS, 64), 0), 2) == iota((SLOTS, 64), 1))
    meta = hot_dot(of_source, first_recv[:, 4:5, :].reshape(64, NB), 2)
    lane, own = iota((SLOTS, NB), 1), iota((SLOTS, NB), 0) & 3
    station = jnp.sum(jnp.where(lane == own, meta, 0.0), axis=1, keepdims=True)
    count = jnp.sum(jnp.where(lane == own + 4, meta, 0.0), axis=1, keepdims=True)
    owner_cols[...] = hot(station == iota((SLOTS, 32), 1).astype(F32))
    owner = owner_cols[...]
    station_count = hot_dot(owner, jnp.broadcast_to(count, (SLOTS, NB)), 2, TN_DIMS)
    terms = [None, None]

    def at_owner(sweep, h):
        if sweep == 0 and h == 0:
            sums = first_recv[:, 0:4, :].reshape(SLOTS, NB)
        else:
            slot = sweep * 2 + h - 1
            arrived(1 if sweep == 0 else 4 + h, sum_recv.at[slot])
            sums = sum_recv[slot]
        terms[h] = hot_dot(owner, sums, 3, TN_DIMS) / station_count
        slot = sweep * 2 + h
        term_send[slot] = hot_dot(owner, terms[h])
        exchange_rows(2 + sweep * 4 + h, term_send.at[slot], term_recv.at[slot])

    def at_source(h):
        arrived(2 + h, term_recv.at[h])
        shot_terms[h] = (shot_sums[h] - hot_dot(counts, term_recv[h])) / shot_count
        sum_send[1 + h] = slot_sums[h] - hot_dot(counts_t, shot_terms[h])
        exchange_rows(4 + h, sum_send.at[1 + h], sum_recv.at[1 + h])

    at_owner(0, 0)
    at_owner(0, 1)
    for c in range(4):
        rows = slice(c * 512, (c + 1) * 512)
        owner_lane = owner_idx[...]
        local_lane = local_idx[...]
        place = (owner_lane & 1) * 1024 + lax.shift_right_logical(local_lane, 4) * 512 + (
            lax.shift_right_logical(owner_lane, 1) & 3) * 128 + lax.shift_right_logical(owner_lane, 3) * 16 + (local_lane & 15)
        cmp_hot[rows, :] = hot(iota((512, TDEV), 0) + c * 512 == place)
    at_source(0)
    at_source(1)
    at_owner(1, 0)
    at_owner(1, 1)

    k0, k1 = iota((256, 256), 0), iota((256, 256), 1)
    order = hot(k1 == 2 * (k0 & 127) + lax.shift_right_logical(k0, 7))

    def ordered(even, odd):
        total = jnp.zeros((even.shape[0], 256), F32)
        for piece in split(jnp.concatenate([even, odd], axis=1), 3):
            total = total + jnp.dot(piece, order, preferred_element_type=F32)
        return total

    out[0:16, :] = ordered(shot_terms[0], shot_terms[1])
    out[16:48, :] = ordered(terms[0], terms[1])
    shot_part = [hot_dot(shot_cols[...], shot_terms[h]) for h in range(2)]
    ones = jnp.ones((8, NB), BF16)
    partial = jnp.zeros((8, TDEV), F32)
    for h in range(2):
        arrived(6 + h, term_recv.at[2 + h])
        root = jnp.exp(0.5 * (shot_part[h] + hot_dot(slot_cols[...], term_recv[2 + h])))
        roots[h] = root
        for piece in split(root * root, 3):
            partial = partial + lax.dot_general(ones, piece, NT_DIMS, preferred_element_type=F32)
    q_send[...] = partial[0:1, :]
    q_recv[band] = partial[0:1, :]
    q_copies = []
    for p in (2, 1, 3):
        copy = pltpu.make_async_remote_copy(
            src_ref=q_send, dst_ref=q_recv.at[band], send_sem=q_ssem.at[p - 1], recv_sem=q_rsem.at[p - 1],
            device_id={"freq": lax.rem(band + p, 4)},
        )
        copy.start()
        q_copies.append(copy)
    for copy in q_copies:
        copy.wait()
    total = (q_recv[0] + q_recv[1]) + (q_recv[2] + q_recv[3])
    floor = jnp.transpose(jnp.broadcast_to(total, (8, TDEV)))[:, 0:1] * (0.3 / 1024.0)
    floor = jnp.broadcast_to(floor, (TDEV, NB))
    for h in range(2):
        root = roots[h]
        wiener = root / (root * root + floor)
        for c in range(2):
            cols = slice((2 * h + c) * NB, (2 * h + c + 1) * NB)
            spec[:, cols] = wiener * spec[:, cols]

    sibling = {"trace": me + 1 - 2 * core}

    def part_rows(of_core, c):
        return pl.ds(pl.multiple_of(of_core * 1024 + (c % 2) * 512, 512), 512)

    def stack(g, rows):
        parts = jnp.concatenate(split(spec[:, g * NB:(g + 1) * NB], 2), axis=1)
        full = jnp.dot(cmp_hot[rows, :], parts, preferred_element_type=F32)
        return full[:, :NB] + full[:, NB:]

    def at_x(step):
        return {"trace": z * 8 + lax.rem(x + step, 4) * 2 + core}

    def x_rows(c, step, first, size):
        return pl.ds(pl.multiple_of(core * 1024 + (c % 2) * 512 + lax.rem(x + step, 4) * 128 + first, 64), size)

    def send(src, dst, stage, sem, to):
        return pltpu.make_async_remote_copy(
            src_ref=src, dst_ref=dst, send_sem=rs_send.at[stage], recv_sem=sem, device_id=to
        )

    def step0(c):
        return send(dense.at[c // 2, part_rows(1 - core, c)], rs0.at[c], 0, rs0_sem.at[c], sibling)

    def step1(c, d):
        return send(dense.at[c // 2, x_rows(c, 2, 64 * d, 64)], rs1.at[c, d], 1, rs1_sem.at[c, d], at_x(1 + 2 * d))

    def step2(c, d):
        return send(dense.at[c // 2, x_rows(c, 1 + 2 * d, 0, 128)], rs2.at[c, d], 2, rs2_sem.at[c, d], at_x(1 + 2 * d))

    def begin(c):
        g = c // 2
        dense[g, part_rows(1 - core, c), :] = stack(g, part_rows(1 - core, c))
        step0(c).start()
        dense[g, part_rows(core, c), :] = stack(g, part_rows(core, c))

    def after0(c):
        g, rows = c // 2, part_rows(core, c)
        step0(c).wait_recv()
        dense[g, rows, :] = dense[g, rows, :] + rs0[c]
        for d in range(2):
            step1(c, d).start()

    def after1(c):
        g = c // 2
        for d in range(2):
            step1(c, d).wait_recv()
            rows = x_rows(c, 1 + 2 * d, 64 * d, 64)
            dense[g, rows, :] = dense[g, rows, :] + rs1[c, d]
            step2(c, d).start()

    def after2(c):
        g, mine = c // 2, x_rows(c, 0, 0, 128)
        for d in range(2):
            step2(c, d).wait_recv()
        dense[g, mine, :] = dense[g, mine, :] + (rs2[c, 0] + rs2[c, 1])
        own = pl.ds(pl.multiple_of(z * 16, 16), 16)
        first = core * 1024 + (c % 2) * 512 + x * 128
        rs3[c, own, :] = dense[g, pl.ds(pl.multiple_of(first + z * 16, 16), 16), :]
        for p in (4, 3, 5, 2, 6, 1, 7):
            there = lax.rem(z + p, 8)
            send(
                dense.at[g, pl.ds(pl.multiple_of(first + there * 16, 16), 16)], rs3.at[c, own],
                3, rs3_sem.at[c], {"trace": there * 8 + x * 2 + core},
            ).start()

    def after3(c):
        rows = pl.ds(0, 112)
        pltpu.make_async_copy(rs3.at[c, rows], rs3.at[c, rows], rs3_sem.at[c]).wait()
        total = rs3[c, 0:16, :]
        for s in range(1, 8):
            total = total + rs3[c, s * 16:(s + 1) * 16, :]
        stacked[c // 2, (c % 2) * 16:(c % 2 + 1) * 16, :] = 0.25 * total

    for step in range(12):
        for offset, stage in ((0, begin), (1, after0), (2, after1), (3, after2), (4, after3)):
            if 0 <= step - offset < 8:
                stage(step - offset)

    for part in range(2):
        out[48 + 32 * part:80 + 32 * part, :] = ordered(stacked[part], stacked[2 + part])
    for stage, ref in (
        (0, dense.at[:, pl.ds(0, 1024)]), (1, dense.at[:, pl.ds(0, 256)]),
        (2, dense.at[:, pl.ds(0, 512)]), (3, dense.at[:, pl.ds(0, 224)]),
    ):
        pending.append(pltpu.make_async_copy(ref, ref, rs_send.at[stage]).wait)
    for wait in pending:
        wait()


def shards(low_tab, high_tab, traces, shot_local, rec_slot, slot_station, cmp_owner, cmp_local):
    vmem = pltpu.VMEM
    dma = pltpu.SemaphoreType.DMA
    i32 = jnp.int32
    out = pl.pallas_call(
        kernel,
        out_shape=jax.ShapeDtypeStruct((112, 256), F32),
        in_specs=[pl.BlockSpec(memory_space=pl.ANY)] * 8,
        out_specs=pl.BlockSpec(memory_space=vmem),
        scratch_shapes=[
            vmem((TDEV, NT), F32), vmem((2, 128, 256), F32), vmem((2, 8, 256), F32), vmem((2, HALF, 512), BF16),
            vmem((TDEV, HALF), BF16), vmem((TDEV, HALF), BF16), vmem((TDEV, HALF), BF16), vmem((TDEV, HALF), BF16),
            vmem((TDEV, NB), F32), vmem((TDEV, 512), F32), vmem((2, TDEV, NB), F32), vmem((2, TDEV, NB), F32),
            vmem((1, TDEV), i32), vmem((1, TDEV), i32), vmem((1, SLOTS), i32), vmem((1, TDEV), i32), vmem((1, TDEV), i32),
            vmem((SLOTS, TDEV), BF16), vmem((TDEV, SLOTS), BF16), vmem((TDEV, 16), BF16),
            vmem((2048, TDEV), BF16), vmem((SLOTS, 32), BF16),
            vmem((64, 8, NB), F32), vmem((64, 8, NB), F32),
            vmem((3, SLOTS, NB), F32), vmem((3, SLOTS, NB), F32), vmem((4, SLOTS, NB), F32), vmem((4, SLOTS, NB), F32),
            vmem((1, TDEV), F32), vmem((4, 1, TDEV), F32),
            vmem((4, 2048, NB), F32), vmem((8, 512, NB), F32), vmem((8, 2, 64, NB), F32),
            vmem((8, 2, 128, NB), F32), vmem((8, 128, NB), F32), vmem((4, 32, NB), F32),
            dma((8,)), dma((2,)), dma((5,)), dma((8,)), dma((8,)), dma((3,)), dma((3,)),
            dma((4,)), dma((8,)), dma((8, 2)), dma((8, 2)), dma((8,)),
        ],
        compiler_params=pltpu.CompilerParams(
            collective_id=0, has_side_effects=True, vmem_limit_bytes=56 * 1024 * 1024
        ),
    )(
        traces, shot_local, rec_slot, slot_station, cmp_owner.reshape(1, TDEV), cmp_local.reshape(1, TDEV),
        low_tab, high_tab,
    )
    return out[0:16], out[16:48], jnp.stack([out[48:80], out[80:112]], axis=1)


def solution(mesh):
    low, high = twiddles()
    body = jax.shard_map(
        shards,
        mesh=mesh,
        in_specs=(
            P(), P(),
            P("trace", None),
            P("trace", None),
            P("trace", None),
            P("trace", None),
            P("trace", None),
            P("trace"),
        ),
        out_specs=(P("trace", "freq"), P("trace", "freq"), P("trace", None, "freq")),
        check_vma=False,
    )
    return functools.partial(body, low, high)
```

time: 102 us -> 92.3 us (0.905); the launches traced: 101 us -> 92.1 us
  Pallas kernels: 93.3 us -> 88 us
  local copies, waits for them, and re-layouts: 5.34 us -> 3.42 us
  other arithmetic: 1.47 us -> 0.01 us
    pallas_call x1, Pallas kernels: 93.3 us -> 88 us  [shards(): pl.pallas_call(kernel, out_shape=jax.ShapeDtypeStruct((112, 256), F32), i...]
    unnamed x3 -> x1, local copies, waits for them, and re-layouts: 2.11 us -> 0.68 us
    slice x0 -> x1, local copies, waits for them, and re-layouts: none -> 1.32 us  [shards(): return (out[0:16], out[16:48], jnp.stack([out[48:80], out[80:112]], axis=1))]
    another operation x6 -> x1, local copies, waits for them, and re-layouts: 2.62 us -> 1.41 us  [shards(): return (out[0:16], out[16:48], jnp.stack([out[48:80], out[80:112]], axis=1))]
where the time goes in v2:
time: 92.3 us; the launch traced here: 92.1 us
  Pallas kernels  88 us (95%)
  local copies, waits for them, and re-layouts  3.42 us (4%)
    pallas_call x1, Pallas kernels, shards(): pl.pallas_call(kernel, out_shape=jax.ShapeDtypeStruct((112, 256), F32), i...  88 us

profile of v2, /device:TPU:32, one launch (start us, length us, event | category | flops | bytes accessed | tf_op | source)
XLA Modules:
  0.0 92.1 jit_solution(13842622071485548904)
XLA Ops:
  0.6 88.0 %shard_map.103 = f32[112,256]{1,0:T(8,128)} custom-call(f32[512,2048]{1,0:T(8,128)} %traces.1, s32[1,512]{1,0:T(1,128)} %shot_in.1, s32[1,512]{1,0:T(1,128)} %slot_in.1, s32[1,256]{1,0:T(1,128)} %station_in.1, s32[1,512]{1,0:T(1,128)} %bitcast.6, s32[1,512]{1,0:T(1,128)} %bitcast.7, f32[4,2,128,256]{3,2,1,0:T(8,128)} %constant.4.clone.low_tab, ...), custom_call_target="tpu_custom_call" | custom-call | tf_op jit(solution)/shard_map/pallas_call | solution.py:396
  88.7 1.3 %slice.12 = f32[16,256]{1,0:T(8,128)} slice(f32[112,256]{1,0:T(8,128)} %shard_map.103), slice={[0:16], [0:256]} | slice | bytes 32768 | tf_op jit(solution)/shard_map/slice | solution.py:423
  90.0 1.4 %slice_bitcast_fusion.1 = (f32[32,1,256]{2,0,1:T(8,128)S(1)}, f32[32,1,256]{2,0,1:T(8,128)S(1)}, f32[32,256]{1,0:T(8,128)}) fusion(f32[112,256]{1,0:T(8,128)} %shard_map.103), kind=kLoop, calls=%fused_computation.2 | loop fusion | bytes 196608 | tf_op jit(solution)/shard_map/stack | solution.py:423
  91.4 0.7 copy.11
  (1 shorter events, 0.0 us)

commit v3 on v2

--- a/solution.py
+++ b/solution.py
@@ -58,13 +58,13 @@
 
 def kernel(
     traces, shot_in, slot_in, station_in, owner_in, local_in, low_tab, high_tab,
-    out,
+    shot_out, rec_out, cmp_out,
     xbuf, low, high, table, uhi, ulo, vhi, vlo, level, spec, logs, roots,
     shot_idx, slot_idx, station_idx, owner_idx, local_idx,
     slot_rows, slot_cols, shot_cols, cmp_hot, owner_cols,
     first_send, first_recv, sum_send, sum_recv, term_send, term_recv, q_send, q_recv,
-    dense, rs0, rs1, rs2, rs3, stacked,
-    x_sem, tab_sem, idx_sem, a2a_send, a2a_recv, q_ssem, q_rsem, rs_send, rs0_sem, rs1_sem, rs2_sem, rs3_sem,
+    dense, rs0, rs1, rs2, rs3, rsz, zsum, rsx, stacked,
+    x_sem, tab_sem, idx_sem, a2a_send, a2a_recv, q_ssem, q_rsem, rs0_sem, rs1_sem, rs2_sem, rs3_sem, rsz_sem, rsx_sem,
 ):
     me = lax.axis_index("trace")
     band = lax.axis_index("freq")
@@ -266,8 +266,8 @@
             total = total + jnp.dot(piece, order, preferred_element_type=F32)
         return total
 
-    out[0:16, :] = ordered(shot_terms[0], shot_terms[1])
-    out[16:48, :] = ordered(terms[0], terms[1])
+    shot_out[...] = ordered(shot_terms[0], shot_terms[1])
+    rec_out[...] = ordered(terms[0], terms[1])
     shot_part = [hot_dot(shot_cols[...], shot_terms[h]) for h in range(2)]
     ones = jnp.ones((8, NB), BF16)
     partial = jnp.zeros((8, TDEV), F32)
@@ -292,112 +292,204 @@
     total = (q_recv[0] + q_recv[1]) + (q_recv[2] + q_recv[3])
     floor = jnp.transpose(jnp.broadcast_to(total, (8, TDEV)))[:, 0:1] * (0.3 / 1024.0)
     floor = jnp.broadcast_to(floor, (TDEV, NB))
-    for h in range(2):
+    def deconvolve(h):
         root = roots[h]
         wiener = root / (root * root + floor)
         for c in range(2):
             cols = slice((2 * h + c) * NB, (2 * h + c + 1) * NB)
             spec[:, cols] = wiener * spec[:, cols]
 
+
     sibling = {"trace": me + 1 - 2 * core}
 
-    def part_rows(of_core, c):
-        return pl.ds(pl.multiple_of(of_core * 1024 + (c % 2) * 512, 512), 512)
-
-    def stack(g, rows):
+    def at_x(step):
+        return {"trace": z * 8 + lax.rem(x + step, 4) * 2 + core}
+
+    def at_z(step):
+        return {"trace": lax.rem(z + step, 8) * 8 + x * 2 + core}
+
+    def send(src, dst, sems, at, to):
+        return pltpu.make_async_remote_copy(
+            src_ref=src, dst_ref=dst, send_sem=sems.at[(0, *at)], recv_sem=sems.at[(1, *at)], device_id=to
+        )
+
+    pieces = ((0, 0, 2), (1, 1, 1), (2, 0, 2), (3, 0, 2), (1, 0, 1))
+
+    def stack(i, of_core):
+        g, first, size = pieces[i]
+        rows = pl.ds(pl.multiple_of(of_core * 1024 + first * 512, 512), size * 512)
         parts = jnp.concatenate(split(spec[:, g * NB:(g + 1) * NB], 2), axis=1)
         full = jnp.dot(cmp_hot[rows, :], parts, preferred_element_type=F32)
-        return full[:, :NB] + full[:, NB:]
-
-    def at_x(step):
-        return {"trace": z * 8 + lax.rem(x + step, 4) * 2 + core}
-
-    def x_rows(c, step, first, size):
-        return pl.ds(pl.multiple_of(core * 1024 + (c % 2) * 512 + lax.rem(x + step, 4) * 128 + first, 64), size)
-
-    def send(src, dst, stage, sem, to):
-        return pltpu.make_async_remote_copy(
-            src_ref=src, dst_ref=dst, send_sem=rs_send.at[stage], recv_sem=sem, device_id=to
+        value = (full[:, :NB] + full[:, NB:]).reshape(size, 4, 8, 16, NB)
+        dense[g, of_core, first:first + size] = value
+
+    def step0(i):
+        g, first, size = pieces[i]
+        half = pl.ds(first, size)
+        return send(dense.at[g, 1 - core, half], rs0.at[g, half], rs0_sem, (i,), sibling)
+
+    def begin(i):
+        stack(i, 1 - core)
+        step0(i).start()
+        stack(i, core)
+
+    def join(i):
+        g, first, size = pieces[i]
+        step0(i).wait_recv()
+        dense[g, core, first:first + size] = dense[g, core, first:first + size] + rs0[g, first:first + size]
+
+    def far(g, size, step, d):
+        if size == 2:
+            return dense.at[g, core, d, lax.rem(x + step, 4)]
+        return dense.at[g, core, 0, lax.rem(x + step, 4), pl.ds(4 * d, 4)]
+
+    def step1(i, d):
+        g, first, size = pieces[i]
+        dst = rs1.at[g, d] if size == 2 else rs1.at[g, d, pl.ds(0, 4)]
+        return send(far(g, size, 2, d), dst, rs1_sem, (i, d), at_x(1 + 2 * d))
+
+    def step2(i, d):
+        g, first, size = pieces[i]
+        half = pl.ds(0, size)
+        return send(
+            dense.at[g, core, half, lax.rem(x + 1 + 2 * d, 4)], rs2.at[g, d, half], rs2_sem, (i, d), at_x(1 + 2 * d)
         )
 
-    def step0(c):
-        return send(dense.at[c // 2, part_rows(1 - core, c)], rs0.at[c], 0, rs0_sem.at[c], sibling)
-
-    def step1(c, d):
-        return send(dense.at[c // 2, x_rows(c, 2, 64 * d, 64)], rs1.at[c, d], 1, rs1_sem.at[c, d], at_x(1 + 2 * d))
-
-    def step2(c, d):
-        return send(dense.at[c // 2, x_rows(c, 1 + 2 * d, 0, 128)], rs2.at[c, d], 2, rs2_sem.at[c, d], at_x(1 + 2 * d))
-
-    def begin(c):
-        g = c // 2
-        dense[g, part_rows(1 - core, c), :] = stack(g, part_rows(1 - core, c))
-        step0(c).start()
-        dense[g, part_rows(core, c), :] = stack(g, part_rows(core, c))
-
-    def after0(c):
-        g, rows = c // 2, part_rows(core, c)
-        step0(c).wait_recv()
-        dense[g, rows, :] = dense[g, rows, :] + rs0[c]
+    def after0(i):
+        join(i)
         for d in range(2):
-            step1(c, d).start()
-
-    def after1(c):
-        g = c // 2
+            step1(i, d).start()
+
+    def after1(i):
+        g, first, size = pieces[i]
         for d in range(2):
-            step1(c, d).wait_recv()
-            rows = x_rows(c, 1 + 2 * d, 64 * d, 64)
-            dense[g, rows, :] = dense[g, rows, :] + rs1[c, d]
-            step2(c, d).start()
-
-    def after2(c):
-        g, mine = c // 2, x_rows(c, 0, 0, 128)
+            step1(i, d).wait_recv()
+            there = lax.rem(x + 1 + 2 * d, 4)
+            if size == 2:
+                dense[g, core, d, there] = dense[g, core, d, there] + rs1[g, d]
+            else:
+                rows = slice(4 * d, 4 * d + 4)
+                dense[g, core, 0, there, rows] = dense[g, core, 0, there, rows] + rs1[g, d, 0:4]
+            step2(i, d).start()
+
+    def step3(i, p):
+        g, first, size = pieces[i]
+        half = pl.ds(0, size)
+        return send(
+            dense.at[g, core, half, x, lax.rem(z + p, 8)], rs3.at[g, z, half], rs3_sem, (i, p - 1), at_z(p)
+        )
+
+    def after2(i):
+        g, first, size = pieces[i]
         for d in range(2):
-            step2(c, d).wait_recv()
-        dense[g, mine, :] = dense[g, mine, :] + (rs2[c, 0] + rs2[c, 1])
-        own = pl.ds(pl.multiple_of(z * 16, 16), 16)
-        first = core * 1024 + (c % 2) * 512 + x * 128
-        rs3[c, own, :] = dense[g, pl.ds(pl.multiple_of(first + z * 16, 16), 16), :]
+            step2(i, d).wait_recv()
+        dense[g, core, 0:size, x] = dense[g, core, 0:size, x] + (rs2[g, 0, 0:size] + rs2[g, 1, 0:size])
         for p in (4, 3, 5, 2, 6, 1, 7):
-            there = lax.rem(z + p, 8)
-            send(
-                dense.at[g, pl.ds(pl.multiple_of(first + there * 16, 16), 16)], rs3.at[c, own],
-                3, rs3_sem.at[c], {"trace": there * 8 + x * 2 + core},
-            ).start()
-
-    def after3(c):
-        rows = pl.ds(0, 112)
-        pltpu.make_async_copy(rs3.at[c, rows], rs3.at[c, rows], rs3_sem.at[c]).wait()
-        total = rs3[c, 0:16, :]
-        for s in range(1, 8):
-            total = total + rs3[c, s * 16:(s + 1) * 16, :]
-        stacked[c // 2, (c % 2) * 16:(c % 2 + 1) * 16, :] = 0.25 * total
-
-    for step in range(12):
-        for offset, stage in ((0, begin), (1, after0), (2, after1), (3, after2), (4, after3)):
-            if 0 <= step - offset < 8:
-                stage(step - offset)
-
-    for part in range(2):
-        out[48 + 32 * part:80 + 32 * part, :] = ordered(stacked[part], stacked[2 + part])
-    for stage, ref in (
-        (0, dense.at[:, pl.ds(0, 1024)]), (1, dense.at[:, pl.ds(0, 256)]),
-        (2, dense.at[:, pl.ds(0, 512)]), (3, dense.at[:, pl.ds(0, 224)]),
-    ):
-        pending.append(pltpu.make_async_copy(ref, ref, rs_send.at[stage]).wait)
+            step3(i, p).start()
+        rs3[g, z, 0:size] = dense[g, core, 0:size, x, z]
+
+    def after3(i):
+        g, first, size = pieces[i]
+        for p in range(1, 8):
+            step3(i, p).wait_recv()
+        total = rs3[g, 0, 0:size]
+        for source in range(1, 8):
+            total = total + rs3[g, source, 0:size]
+        stacked[g, 0:16 * size, :] = 0.25 * total.reshape(16 * size, NB)
+
+    def z_first(p):
+        return send(dense.at[1, core, 1, :, lax.rem(z + p, 8)], rsz.at[z], rsz_sem, (p - 1,), at_z(p))
+
+    def x_last(p):
+        return send(zsum.at[lax.rem(x + p, 4)], rsx.at[x], rsx_sem, (p - 1,), at_x(p))
+
+    def side0():
+        join(1)
+        for p in (4, 3, 5, 2, 6, 1, 7):
+            z_first(p).start()
+        rsz[z] = dense[1, core, 1, :, z]
+
+    def side1():
+        for p in range(1, 8):
+            z_first(p).wait_recv()
+        total = rsz[0]
+        for source in range(1, 8):
+            total = total + rsz[source]
+        zsum[...] = total
+        for p in (2, 1, 3):
+            x_last(p).start()
+        rsx[x] = zsum[x]
+
+    def side2():
+        for p in range(1, 4):
+            x_last(p).wait_recv()
+        stacked[1, 16:32, :] = 0.25 * ((rsx[0] + rsx[1]) + (rsx[2] + rsx[3]))
+
+    deconvolve(0)
+    begin(0)
+    begin(1)
+    after0(0)
+    deconvolve(1)
+    begin(2)
+    side0()
+    after0(2)
+    after1(0)
+    begin(3)
+    after0(3)
+    after1(2)
+    begin(4)
+    after0(4)
+    after2(0)
+    after1(3)
+    side1()
+    after1(4)
+    after2(2)
+    after3(0)
+    after2(3)
+    side2()
+    after3(2)
+    cmp_out[:, 0, :] = ordered(stacked[0], stacked[2])
+    after2(4)
+    after3(3)
+    after3(4)
+    cmp_out[:, 1, :] = ordered(stacked[1], stacked[3])
+
+    for i in range(5):
+        pending.append(step0(i).wait_send)
+    for i in (0, 2, 3, 4):
+        for d in range(2):
+            pending.append(step1(i, d).wait_send)
+            pending.append(step2(i, d).wait_send)
+        for p in range(1, 8):
+            pending.append(step3(i, p).wait_send)
+    for p in range(1, 8):
+        pending.append(z_first(p).wait_send)
+    for p in range(1, 4):
+        pending.append(x_last(p).wait_send)
     for wait in pending:
         wait()
+
+
+def copy_kernel(a, b, c, x, y, z):
+    x[...] = a[...]
+    y[...] = b[...]
+    z[...] = c[...]
 
 
 def shards(low_tab, high_tab, traces, shot_local, rec_slot, slot_station, cmp_owner, cmp_local):
     vmem = pltpu.VMEM
     dma = pltpu.SemaphoreType.DMA
     i32 = jnp.int32
-    out = pl.pallas_call(
+    outs = (
+        jax.ShapeDtypeStruct((16, 256), F32),
+        jax.ShapeDtypeStruct((32, 256), F32),
+        jax.ShapeDtypeStruct((32, 2, 256), F32),
+    )
+    results = pl.pallas_call(
         kernel,
-        out_shape=jax.ShapeDtypeStruct((112, 256), F32),
+        out_shape=outs,
         in_specs=[pl.BlockSpec(memory_space=pl.ANY)] * 8,
-        out_specs=pl.BlockSpec(memory_space=vmem),
+        out_specs=(pl.BlockSpec(memory_space=vmem),) * 3,
         scratch_shapes=[
             vmem((TDEV, NT), F32), vmem((2, 128, 256), F32), vmem((2, 8, 256), F32), vmem((2, HALF, 512), BF16),
             vmem((TDEV, HALF), BF16), vmem((TDEV, HALF), BF16), vmem((TDEV, HALF), BF16), vmem((TDEV, HALF), BF16),
@@ -408,10 +500,11 @@
             vmem((64, 8, NB), F32), vmem((64, 8, NB), F32),
             vmem((3, SLOTS, NB), F32), vmem((3, SLOTS, NB), F32), vmem((4, SLOTS, NB), F32), vmem((4, SLOTS, NB), F32),
             vmem((1, TDEV), F32), vmem((4, 1, TDEV), F32),
-            vmem((4, 2048, NB), F32), vmem((8, 512, NB), F32), vmem((8, 2, 64, NB), F32),
-            vmem((8, 2, 128, NB), F32), vmem((8, 128, NB), F32), vmem((4, 32, NB), F32),
+            vmem((4, 2, 2, 4, 8, 16, NB), F32), vmem((4, 2, 4, 8, 16, NB), F32), vmem((4, 2, 8, 16, NB), F32),
+            vmem((4, 2, 2, 8, 16, NB), F32), vmem((4, 8, 2, 16, NB), F32),
+            vmem((8, 4, 16, NB), F32), vmem((4, 16, NB), F32), vmem((4, 16, NB), F32), vmem((4, 32, NB), F32),
             dma((8,)), dma((2,)), dma((5,)), dma((8,)), dma((8,)), dma((3,)), dma((3,)),
-            dma((4,)), dma((8,)), dma((8, 2)), dma((8, 2)), dma((8,)),
+            dma((2, 5)), dma((2, 5, 2)), dma((2, 5, 2)), dma((2, 5, 7)), dma((2, 7)), dma((2, 3)),
         ],
         compiler_params=pltpu.CompilerParams(
             collective_id=0, has_side_effects=True, vmem_limit_bytes=56 * 1024 * 1024
@@ -420,7 +513,12 @@
         traces, shot_local, rec_slot, slot_station, cmp_owner.reshape(1, TDEV), cmp_local.reshape(1, TDEV),
         low_tab, high_tab,
     )
-    return out[0:16], out[16:48], jnp.stack([out[48:80], out[80:112]], axis=1)
+    return tuple(pl.pallas_call(
+        copy_kernel,
+        out_shape=outs,
+        in_specs=[pl.BlockSpec(memory_space=vmem)] * 3,
+        out_specs=(pl.BlockSpec(memory_space=vmem),) * 3,
+    )(*results))
 
 
 def solution(mesh):

time: 92.3 us -> 81.7 us (0.89)
  Pallas kernels: 88 us -> 80.5 us
  local copies, waits for them, and re-layouts: 3.42 us -> 0 us
    pallas_call x1 -> x2, Pallas kernels: 88 us -> 80.5 us  [the longest x1 78.9 us: shards(): pl.pallas_call(kernel, out_shape=outs, in_specs=[pl.BlockSpec(memory_spac...]
    another operation x1 -> x0, local copies, waits for them, and re-layouts: 1.41 us -> none  [shards(): return (out[0:16], out[16:48], jnp.stack([out[48:80], out[80:112]], axis=1))]
    slice x1 -> x0, local copies, waits for them, and re-layouts: 1.32 us -> none  [shards(): return (out[0:16], out[16:48], jnp.stack([out[48:80], out[80:112]], axis=1))]
where the time goes in v3:
time: 81.7 us; the launch traced here: 81.1 us
  Pallas kernels  80.5 us (99%)
    pallas_call x1, Pallas kernels, shards(): pl.pallas_call(kernel, out_shape=outs, in_specs=[pl.BlockSpec(memory_spac...  78.9 us

profile of v3, /device:TPU:32, one launch (start us, length us, event | category | flops | bytes accessed | tf_op | source)
XLA Modules:
  0.0 81.1 jit_solution(8207475303222008013)
XLA Ops:
  0.6 78.9 %shard_map.103 = (f32[16,256]{1,0:T(8,128)}, f32[32,256]{1,0:T(8,128)}, f32[32,2,256]{2,1,0:T(2,128)}) custom-call(f32[512,2048]{1,0:T(8,128)} %traces.1, s32[1,512]{1,0:T(1,128)} %shot_in.1, s32[1,512]{1,0:T(1,128)} %slot_in.1, s32[1,256]{1,0:T(1,128)} %station_in.1, s32[1,512]{1,0:T(1,128)} %bitcast.2, s32[1,512]{1,0:T(1,128)} %bitcast.3, ...), custom_call_target="tpu_custom_call" | custom-call | tf_op jit(solution)/shard_map/pallas_call | solution.py:488
  79.6 1.5 %shard_map.104 = (f32[16,256]{1,0:T(8,128)}, f32[32,256]{1,0:T(8,128)}, f32[32,2,256]{2,1,0:T(2,128)}) custom-call(f32[16,256]{1,0:T(8,128)} %get-tuple-element.6.a, f32[32,256]{1,0:T(8,128)} %get-tuple-element.7.b, f32[32,2,256]{2,1,0:T(2,128)} %get-tuple-element.8.c), custom_call_target="tpu_custom_call" | custom-call | tf_op jit(solution)/shard_map/pallas_call | solution.py:516

commit v4 on v3

--- a/solution.py
+++ b/solution.py
@@ -63,8 +63,8 @@
     shot_idx, slot_idx, station_idx, owner_idx, local_idx,
     slot_rows, slot_cols, shot_cols, cmp_hot, owner_cols,
     first_send, first_recv, sum_send, sum_recv, term_send, term_recv, q_send, q_recv,
-    dense, rs0, rs1, rs2, rs3, rsz, zsum, rsx, stacked,
-    x_sem, tab_sem, idx_sem, a2a_send, a2a_recv, q_ssem, q_rsem, rs0_sem, rs1_sem, rs2_sem, rs3_sem, rsz_sem, rsx_sem,
+    dense, rs0, rs1, rs2, rs3, rsz, zsum, rsx, stacked, shot_buf, rec_buf, cmp_buf,
+    x_sem, tab_sem, idx_sem, a2a_send, a2a_recv, q_ssem, q_rsem, rs0_sem, rs1_sem, rs2_sem, rs3_sem, rsz_sem, rsx_sem, out_sem,
 ):
     me = lax.axis_index("trace")
     band = lax.axis_index("freq")
@@ -101,7 +101,7 @@
     for p in range(1, 4):
         pl.semaphore_signal(barrier, inc=1, device_id={"freq": lax.rem(band + p, 4)})
 
-    def exchange(leg, source_of, target):
+    def exchange(leg, source_of, target, beside=None):
         sems = dict(send_sem=a2a_send.at[leg], recv_sem=a2a_recv.at[leg])
 
         def put(other):
@@ -116,12 +116,16 @@
             for dx in (2, 1, 3, 0):
                 for dc in (1, 0):
                     put(there + lax.rem(x + dx, 4) * 2 + lax.rem(core + dc, 2))
+            if beside is not None:
+                beside(k)
 
         for dx in (2, 1, 3, 0):
             for dc in (1, 0):
                 if dx or dc:
                     put(z * 8 + lax.rem(x + dx, 4) * 2 + lax.rem(core + dc, 2))
         pltpu.make_async_copy(source_of(me), target(me), a2a_recv.at[leg]).start()
+        if beside is not None:
+            beside(7)
 
     def four(ref):
         return lambda d: ref.at[pl.ds(pl.multiple_of(d * 4, 4), 4)]
@@ -184,15 +188,20 @@
         vhi[rows, :], vlo[rows, :] = split(v, 2)
 
     shot_sums, slot_sums, shot_terms = [None, None], [None, None], [None, None]
-    for h, (hi, lo) in enumerate(((uhi, ulo), (vhi, vlo))):
-        for part in range(2):
-            rows = slice(part * 256, (part + 1) * 256)
-            full = jnp.dot(hi[rows, :], table[h], preferred_element_type=F32)
-            rest = jnp.dot(lo[rows, :], table[h, :, :256], preferred_element_type=F32)
-            both = full[:, :256] + (full[:, 256:] + rest)
-            spec[rows, h * 256:(h + 1) * 256] = both
-            re, im = both[:, :NB], both[:, NB:]
-            logs[h, rows, :] = jnp.log(re * re + im * im + level[rows, :])
+    def transform(h, hi, lo, rows):
+        full = jnp.dot(hi[rows, :], table[h], preferred_element_type=F32)
+        rest = jnp.dot(lo[rows, :], table[h, :, :256], preferred_element_type=F32)
+        both = full[:, :256] + (full[:, 256:] + rest)
+        spec[rows, h * 256:(h + 1) * 256] = both
+        re, im = both[:, :NB], both[:, NB:]
+        logs[h, rows, :] = jnp.log(re * re + im * im + level[rows, :])
+
+    def odd_rows(k):
+        transform(1, vhi, vlo, pl.ds(k * 64 if isinstance(k, int) else pl.multiple_of(k * 64, 64), 64))
+
+    for part in range(2):
+        transform(0, uhi, ulo, pl.ds(part * 256, 256))
+    for h in range(2):
         shot_sums[h] = hot_dot(shots, logs[h])
         slot_sums[h] = hot_dot(slot_rows[...], logs[h])
         shot_terms[h] = shot_sums[h] / shot_count
@@ -200,7 +209,7 @@
         if h == 0:
             first_send[:, 0:4, :] = sums.reshape(64, 4, NB)
             pl.semaphore_wait(barrier, 66)
-            exchange(0, five(first_send), five(first_recv))
+            exchange(0, five(first_send), five(first_recv), odd_rows)
             part = first_send.at[pl.ds(0, 63), pl.ds(0, 5)]
             pending.append(pltpu.make_async_copy(part, part, a2a_send.at[0]).wait)
         else:
@@ -266,8 +275,14 @@
             total = total + jnp.dot(piece, order, preferred_element_type=F32)
         return total
 
-    shot_out[...] = ordered(shot_terms[0], shot_terms[1])
-    rec_out[...] = ordered(terms[0], terms[1])
+    shot_buf[...] = ordered(shot_terms[0], shot_terms[1])
+    rec_buf[...] = ordered(terms[0], terms[1])
+    out_copies = [
+        pltpu.make_async_copy(source, target, out_sem.at[i])
+        for i, (source, target) in enumerate(((shot_buf, shot_out), (rec_buf, rec_out), (cmp_buf, cmp_out)))
+    ]
+    out_copies[0].start()
+    out_copies[1].start()
     shot_part = [hot_dot(shot_cols[...], shot_terms[h]) for h in range(2)]
     ones = jnp.ones((8, NB), BF16)
     partial = jnp.zeros((8, TDEV), F32)
@@ -313,7 +328,7 @@
             src_ref=src, dst_ref=dst, send_sem=sems.at[(0, *at)], recv_sem=sems.at[(1, *at)], device_id=to
         )
 
-    pieces = ((0, 0, 2), (1, 1, 1), (2, 0, 2), (3, 0, 2), (1, 0, 1))
+    pieces = ((0, 0, 1), (1, 0, 2), (0, 1, 1), (2, 0, 2), (3, 0, 1), (3, 1, 1))
 
     def stack(i, of_core):
         g, first, size = pieces[i]
@@ -338,19 +353,19 @@
         step0(i).wait_recv()
         dense[g, core, first:first + size] = dense[g, core, first:first + size] + rs0[g, first:first + size]
 
-    def far(g, size, step, d):
+    def far(g, first, size, step, d):
         if size == 2:
             return dense.at[g, core, d, lax.rem(x + step, 4)]
-        return dense.at[g, core, 0, lax.rem(x + step, 4), pl.ds(4 * d, 4)]
+        return dense.at[g, core, first, lax.rem(x + step, 4), pl.ds(4 * d, 4)]
 
     def step1(i, d):
         g, first, size = pieces[i]
-        dst = rs1.at[g, d] if size == 2 else rs1.at[g, d, pl.ds(0, 4)]
-        return send(far(g, size, 2, d), dst, rs1_sem, (i, d), at_x(1 + 2 * d))
+        dst = rs1.at[g, d] if size == 2 else rs1.at[g, d, pl.ds(4 * first, 4)]
+        return send(far(g, first, size, 2, d), dst, rs1_sem, (i, d), at_x(1 + 2 * d))
 
     def step2(i, d):
         g, first, size = pieces[i]
-        half = pl.ds(0, size)
+        half = pl.ds(first, size)
         return send(
             dense.at[g, core, half, lax.rem(x + 1 + 2 * d, 4)], rs2.at[g, d, half], rs2_sem, (i, d), at_x(1 + 2 * d)
         )
@@ -369,111 +384,144 @@
                 dense[g, core, d, there] = dense[g, core, d, there] + rs1[g, d]
             else:
                 rows = slice(4 * d, 4 * d + 4)
-                dense[g, core, 0, there, rows] = dense[g, core, 0, there, rows] + rs1[g, d, 0:4]
+                dense[g, core, first, there, rows] = dense[g, core, first, there, rows] + rs1[g, d, 4 * first:4 * first + 4]
             step2(i, d).start()
 
     def step3(i, p):
         g, first, size = pieces[i]
-        half = pl.ds(0, size)
+        half = pl.ds(first, size)
         return send(
-            dense.at[g, core, half, x, lax.rem(z + p, 8)], rs3.at[g, z, half], rs3_sem, (i, p - 1), at_z(p)
+            dense.at[g, core, half, x, lax.rem(z + p, 8)], rs3.at[g, z, half], rs3_sem, (i,), at_z(p)
         )
 
     def after2(i):
         g, first, size = pieces[i]
         for d in range(2):
             step2(i, d).wait_recv()
-        dense[g, core, 0:size, x] = dense[g, core, 0:size, x] + (rs2[g, 0, 0:size] + rs2[g, 1, 0:size])
+        last = first + size
+        dense[g, core, first:last, x] = dense[g, core, first:last, x] + (rs2[g, 0, first:last] + rs2[g, 1, first:last])
         for p in (4, 3, 5, 2, 6, 1, 7):
             step3(i, p).start()
-        rs3[g, z, 0:size] = dense[g, core, 0:size, x, z]
+        rs3[g, z, first:last] = dense[g, core, first:last, x, z]
+
+    def step3_bytes(i, way):
+        g, first, size = pieces[i]
+        part = rs3.at[g, pl.ds(0, 7), pl.ds(first, size)]
+        return pltpu.make_async_copy(part, part, rs3_sem.at[way, i])
 
     def after3(i):
         g, first, size = pieces[i]
-        for p in range(1, 8):
-            step3(i, p).wait_recv()
-        total = rs3[g, 0, 0:size]
+        last = first + size
+        step3_bytes(i, 1).wait()
+        total = rs3[g, 0, first:last]
         for source in range(1, 8):
-            total = total + rs3[g, source, 0:size]
-        stacked[g, 0:16 * size, :] = 0.25 * total.reshape(16 * size, NB)
-
-    def z_first(p):
-        return send(dense.at[1, core, 1, :, lax.rem(z + p, 8)], rsz.at[z], rsz_sem, (p - 1,), at_z(p))
+            total = total + rs3[g, source, first:last]
+        stacked[g, 16 * first:16 * last, :] = 0.25 * total.reshape(16 * size, NB)
+
+    def round_z(flow, step):
+        there = lax.rem(z + 4 - step, 8) if flow == 0 else lax.rem(z + 5 + step, 8)
+        return send(
+            dense.at[1, core, :, :, there], rsz.at[flow, step], rsz_sem, (flow, step), at_z(1 if flow == 0 else 7)
+        )
 
     def x_last(p):
-        return send(zsum.at[lax.rem(x + p, 4)], rsx.at[x], rsx_sem, (p - 1,), at_x(p))
+        return send(zsum.at[:, lax.rem(x + p, 4)], rsx.at[x], rsx_sem, (p - 1,), at_x(p))
 
     def side0():
         join(1)
-        for p in (4, 3, 5, 2, 6, 1, 7):
-            z_first(p).start()
-        rsz[z] = dense[1, core, 1, :, z]
-
-    def side1():
-        for p in range(1, 8):
-            z_first(p).wait_recv()
-        total = rsz[0]
-        for source in range(1, 8):
-            total = total + rsz[source]
-        zsum[...] = total
+        round_z(0, 0).start()
+        round_z(1, 0).start()
+
+    def side(step):
+        for flow in range(2):
+            if step <= 3:
+                round_z(flow, step - 1).wait_recv()
+                there = lax.rem(z + 4 - step, 8) if flow == 0 else lax.rem(z + 5 + step, 8)
+                dense[1, core, :, :, there] = dense[1, core, :, :, there] + rsz[flow, step - 1]
+                if flow == 0 or step < 3:
+                    round_z(flow, step).start()
+
+    def side4():
+        round_z(0, 3).wait_recv()
+        zsum[...] = dense[1, core, :, :, z] + rsz[0, 3]
         for p in (2, 1, 3):
             x_last(p).start()
-        rsx[x] = zsum[x]
-
-    def side2():
+        rsx[x] = zsum[:, x]
+
+    def side5():
         for p in range(1, 4):
             x_last(p).wait_recv()
-        stacked[1, 16:32, :] = 0.25 * ((rsx[0] + rsx[1]) + (rsx[2] + rsx[3]))
+        stacked[1] = 0.25 * ((rsx[0] + rsx[1]) + (rsx[2] + rsx[3])).reshape(32, NB)
 
     deconvolve(0)
     begin(0)
     begin(1)
     after0(0)
-    deconvolve(1)
     begin(2)
     side0()
+    deconvolve(1)
     after0(2)
+    begin(3)
     after1(0)
-    begin(3)
+    begin(4)
     after0(3)
     after1(2)
-    begin(4)
+    side(1)
+    begin(5)
     after0(4)
     after2(0)
     after1(3)
-    side1()
+    after0(5)
+    after2(2)
+    side(2)
     after1(4)
-    after2(2)
     after3(0)
+    after1(5)
+    side(3)
     after2(3)
-    side2()
     after3(2)
-    cmp_out[:, 0, :] = ordered(stacked[0], stacked[2])
+    side4()
     after2(4)
     after3(3)
-    after3(4)
-    cmp_out[:, 1, :] = ordered(stacked[1], stacked[3])
-
-    for i in range(5):
+    cmp_buf[:, 0, :] = ordered(stacked[0], stacked[2])
+    after2(5)
+    for i in range(6):
         pending.append(step0(i).wait_send)
-    for i in (0, 2, 3, 4):
+    for i in (0, 2, 3, 4, 5):
         for d in range(2):
             pending.append(step1(i, d).wait_send)
             pending.append(step2(i, d).wait_send)
-        for p in range(1, 8):
-            pending.append(step3(i, p).wait_send)
-    for p in range(1, 8):
-        pending.append(z_first(p).wait_send)
+        if i < 5:
+            pending.append(step3_bytes(i, 0).wait)
+    for step in range(4):
+        pending.append(round_z(0, step).wait_send)
+    for step in range(3):
+        pending.append(round_z(1, step).wait_send)
     for p in range(1, 4):
         pending.append(x_last(p).wait_send)
     for wait in pending:
         wait()
-
-
-def copy_kernel(a, b, c, x, y, z):
-    x[...] = a[...]
-    y[...] = b[...]
-    z[...] = c[...]
+    side5()
+    after3(4)
+    after3(5)
+    cmp_buf[:, 1, :] = ordered(stacked[1], stacked[3])
+    out_copies[2].start()
+    step3_bytes(5, 0).wait()
+    for copy in out_copies:
+        copy.wait()
+
+
+def copy_kernel(a, b, c, x, y, z, p, q, r, sems):
+    triples = ((a, p, x), (b, q, y), (c, r, z))
+    reads = [pltpu.make_async_copy(s, m, sems.at[0, i]) for i, (s, m, t) in enumerate(triples)]
+    writes = [pltpu.make_async_copy(m, t, sems.at[1, i]) for i, (s, m, t) in enumerate(triples)]
+    for copy in reads:
+        copy.start()
+    for read, write in zip(reads, writes):
+        read.wait()
+        write.start()
+    for copy in writes:
+        copy.wait()
 
 
 def shards(low_tab, high_tab, traces, shot_local, rec_slot, slot_station, cmp_owner, cmp_local):
@@ -489,7 +537,7 @@
         kernel,
         out_shape=outs,
         in_specs=[pl.BlockSpec(memory_space=pl.ANY)] * 8,
-        out_specs=(pl.BlockSpec(memory_space=vmem),) * 3,
+        out_specs=(pl.BlockSpec(memory_space=pl.ANY),) * 3,
         scratch_shapes=[
             vmem((TDEV, NT), F32), vmem((2, 128, 256), F32), vmem((2, 8, 256), F32), vmem((2, HALF, 512), BF16),
             vmem((TDEV, HALF), BF16), vmem((TDEV, HALF), BF16), vmem((TDEV, HALF), BF16), vmem((TDEV, HALF), BF16),
@@ -502,9 +550,10 @@
             vmem((1, TDEV), F32), vmem((4, 1, TDEV), F32),
             vmem((4, 2, 2, 4, 8, 16, NB), F32), vmem((4, 2, 4, 8, 16, NB), F32), vmem((4, 2, 8, 16, NB), F32),
             vmem((4, 2, 2, 8, 16, NB), F32), vmem((4, 8, 2, 16, NB), F32),
-            vmem((8, 4, 16, NB), F32), vmem((4, 16, NB), F32), vmem((4, 16, NB), F32), vmem((4, 32, NB), F32),
+            vmem((2, 4, 2, 4, 16, NB), F32), vmem((2, 4, 16, NB), F32), vmem((4, 2, 16, NB), F32), vmem((4, 32, NB), F32),
+            vmem((16, 256), F32), vmem((32, 256), F32), vmem((32, 2, 256), F32),
             dma((8,)), dma((2,)), dma((5,)), dma((8,)), dma((8,)), dma((3,)), dma((3,)),
-            dma((2, 5)), dma((2, 5, 2)), dma((2, 5, 2)), dma((2, 5, 7)), dma((2, 7)), dma((2, 3)),
+            dma((2, 6)), dma((2, 6, 2)), dma((2, 6, 2)), dma((2, 6)), dma((2, 2, 4)), dma((2, 3)), dma((3,)),
         ],
         compiler_params=pltpu.CompilerParams(
             collective_id=0, has_side_effects=True, vmem_limit_bytes=56 * 1024 * 1024
@@ -516,8 +565,10 @@
     return tuple(pl.pallas_call(
         copy_kernel,
         out_shape=outs,
-        in_specs=[pl.BlockSpec(memory_space=vmem)] * 3,
-        out_specs=(pl.BlockSpec(memory_space=vmem),) * 3,
+        in_specs=[pl.BlockSpec(memory_space=pl.ANY)] * 3,
+        out_specs=(pl.BlockSpec(memory_space=pl.ANY),) * 3,
+        scratch_shapes=[vmem((16, 256), F32), vmem((32, 256), F32), vmem((32, 2, 256), F32), dma((2, 3))],
+        compiler_params=pltpu.CompilerParams(vmem_limit_bytes=56 * 1024 * 1024),
     )(*results))
 
 

time: 81.7 us -> 80.8 us (0.989)
  Pallas kernels: 80.5 us -> 79.5 us
    pallas_call x1, Pallas kernels: 78.9 us -> 78 us  [shards(): pl.pallas_call(kernel, out_shape=outs, in_specs=[pl.BlockSpec(memory_spac...]
where the time goes in v4:
time: 80.8 us; the launch traced here: 80.2 us
  Pallas kernels  79.5 us (98%)
    pallas_call x1, Pallas kernels, shards(): pl.pallas_call(kernel, out_shape=outs, in_specs=[pl.BlockSpec(memory_spac...  78 us

profile of v4, /device:TPU:32, one launch (start us, length us, event | category | flops | bytes accessed | tf_op | source)
XLA Modules:
  0.0 80.2 jit_solution(4310486632796585996)
XLA Ops:
  0.6 78.0 %shard_map.103 = (f32[16,256]{1,0:T(8,128)}, f32[32,256]{1,0:T(8,128)}, f32[32,2,256]{2,1,0:T(2,128)}) custom-call(f32[512,2048]{1,0:T(8,128)} %traces.1, s32[1,512]{1,0:T(1,128)} %shot_in.1, s32[1,512]{1,0:T(1,128)} %slot_in.1, s32[1,256]{1,0:T(1,128)} %station_in.1, s32[1,512]{1,0:T(1,128)} %bitcast.2, s32[1,512]{1,0:T(1,128)} %bitcast.3, ...), custom_call_target="tpu_custom_call" | custom-call | tf_op jit(solution)/shard_map/pallas_call | solution.py:536
  78.6 1.6 %shard_map.104 = (f32[16,256]{1,0:T(8,128)}, f32[32,256]{1,0:T(8,128)}, f32[32,2,256]{2,1,0:T(2,128)}) custom-call(f32[16,256]{1,0:T(8,128)} %get-tuple-element.6.a, f32[32,256]{1,0:T(8,128)} %get-tuple-element.7.b, f32[32,2,256]{2,1,0:T(2,128)} %get-tuple-element.8.c), custom_call_target="tpu_custom_call" | custom-call | tf_op jit(solution)/shard_map/pallas_call | solution.py:565

commit v5 on v4

--- a/solution.py
+++ b/solution.py
@@ -72,6 +72,7 @@
     x = lax.rem(lax.div(me, 2), 4)
     core = lax.rem(me, 2)
     pending = []
+    places = [lax.rem(x + dx, 4) * 2 + lax.rem(core + dc, 2) for dx in (2, 1, 3, 0) for dc in (1, 0)]
 
     def x_copy(c):
         rows = pl.ds(c * 64, 64)
@@ -113,16 +114,13 @@
         def _(k):
             side = 1 - 2 * lax.rem(k, 2)
             there = lax.rem(z + 12 + side * lax.div(k + 1, 2), 8) * 8
-            for dx in (2, 1, 3, 0):
-                for dc in (1, 0):
-                    put(there + lax.rem(x + dx, 4) * 2 + lax.rem(core + dc, 2))
+            for place in places:
+                put(there + place)
             if beside is not None:
                 beside(k)
 
-        for dx in (2, 1, 3, 0):
-            for dc in (1, 0):
-                if dx or dc:
-                    put(z * 8 + lax.rem(x + dx, 4) * 2 + lax.rem(core + dc, 2))
+        for place in places[:7]:
+            put(z * 8 + place)
         pltpu.make_async_copy(source_of(me), target(me), a2a_recv.at[leg]).start()
         if beside is not None:
             beside(7)
@@ -477,14 +475,14 @@
     after1(4)
     after3(0)
     after1(5)
+    after2(3)
     side(3)
-    after2(3)
+    after2(4)
     after3(2)
-    side4()
-    after2(4)
     after3(3)
     cmp_buf[:, 0, :] = ordered(stacked[0], stacked[2])
     after2(5)
+    side4()
     for i in range(6):
         pending.append(step0(i).wait_send)
     for i in (0, 2, 3, 4, 5):
@@ -501,8 +499,8 @@
         pending.append(x_last(p).wait_send)
     for wait in pending:
         wait()
+    after3(4)
     side5()
-    after3(4)
     after3(5)
     cmp_buf[:, 1, :] = ordered(stacked[1], stacked[3])
     out_copies[2].start()

time: 80.8 us -> 79.3 us (0.981)
  Pallas kernels: 79.5 us -> 78.5 us
    pallas_call x1, Pallas kernels: 78 us -> 76.9 us  [shards(): pl.pallas_call(kernel, out_shape=outs, in_specs=[pl.BlockSpec(memory_spac...]
where the time goes in v5:
time: 79.3 us; the launch traced here: 79.1 us
  Pallas kernels  78.5 us (99%)
    pallas_call x1, Pallas kernels, shards(): pl.pallas_call(kernel, out_shape=outs, in_specs=[pl.BlockSpec(memory_spac...  76.9 us

profile of v5, /device:TPU:32, one launch (start us, length us, event | category | flops | bytes accessed | tf_op | source)
XLA Modules:
  0.0 79.1 jit_solution(1621981883276335459)
XLA Ops:
  0.6 76.9 %shard_map.103 = (f32[16,256]{1,0:T(8,128)}, f32[32,256]{1,0:T(8,128)}, f32[32,2,256]{2,1,0:T(2,128)}) custom-call(f32[512,2048]{1,0:T(8,128)} %traces.1, s32[1,512]{1,0:T(1,128)} %shot_in.1, s32[1,512]{1,0:T(1,128)} %slot_in.1, s32[1,256]{1,0:T(1,128)} %station_in.1, s32[1,512]{1,0:T(1,128)} %bitcast.2, s32[1,512]{1,0:T(1,128)} %bitcast.3, ...), custom_call_target="tpu_custom_call" | custom-call | tf_op jit(solution)/shard_map/pallas_call | solution.py:534
  77.6 1.6 %shard_map.104 = (f32[16,256]{1,0:T(8,128)}, f32[32,256]{1,0:T(8,128)}, f32[32,2,256]{2,1,0:T(2,128)}) custom-call(f32[16,256]{1,0:T(8,128)} %get-tuple-element.6.a, f32[32,256]{1,0:T(8,128)} %get-tuple-element.7.b, f32[32,2,256]{2,1,0:T(2,128)} %get-tuple-element.8.c), custom_call_target="tpu_custom_call" | custom-call | tf_op jit(solution)/shard_map/pallas_call | solution.py:563

commit v6 on v5

--- a/solution.py
+++ b/solution.py
@@ -471,8 +471,8 @@
     after1(3)
     after0(5)
     after2(2)
+    after1(4)
     side(2)
-    after1(4)
     after3(0)
     after1(5)
     after2(3)

time: 79.3 us -> 79.3 us (level)
  no operation moved by 1% of the time
where the time goes in v6:
time: 79.3 us; the launch traced here: 79.1 us
  Pallas kernels  78.5 us (99%)
    pallas_call x1, Pallas kernels, shards(): pl.pallas_call(kernel, out_shape=outs, in_specs=[pl.BlockSpec(memory_spac...  76.9 us

profile of v6, /device:TPU:32, one launch (start us, length us, event | category | flops | bytes accessed | tf_op | source)
XLA Modules:
  0.0 79.1 jit_solution(12052253564116306215)
XLA Ops:
  0.6 76.9 %shard_map.103 = (f32[16,256]{1,0:T(8,128)}, f32[32,256]{1,0:T(8,128)}, f32[32,2,256]{2,1,0:T(2,128)}) custom-call(f32[512,2048]{1,0:T(8,128)} %traces.1, s32[1,512]{1,0:T(1,128)} %shot_in.1, s32[1,512]{1,0:T(1,128)} %slot_in.1, s32[1,256]{1,0:T(1,128)} %station_in.1, s32[1,512]{1,0:T(1,128)} %bitcast.2, s32[1,512]{1,0:T(1,128)} %bitcast.3, ...), custom_call_target="tpu_custom_call" | custom-call | tf_op jit(solution)/shard_map/pallas_call | solution.py:534
  77.6 1.6 %shard_map.104 = (f32[16,256]{1,0:T(8,128)}, f32[32,256]{1,0:T(8,128)}, f32[32,2,256]{2,1,0:T(2,128)}) custom-call(f32[16,256]{1,0:T(8,128)} %get-tuple-element.6.a, f32[32,256]{1,0:T(8,128)} %get-tuple-element.7.b, f32[32,2,256]{2,1,0:T(2,128)} %get-tuple-element.8.c), custom_call_target="tpu_custom_call" | custom-call | tf_op jit(solution)/shard_map/pallas_call | solution.py:563
